TPU v7x, 32 devices: a whole 2x2x4 slice. The times are simulated.
32 devices in a mesh: dp: 4 (over y, core), fsdp: 8 (over z, x).
Axes of the slice: x: 2, y: 2, z: 4, core: 2. Of those that a mesh axis runs over, the one named last changes fastest.
Arguments:
- tokens: bfloat16 [8, 1536, 1408], P('fsdp', 'dp')
- patches: int32 [8, 4, 4], P('fsdp', 'dp'), may hold values from 1 to 192, as said below
- owners: int32 [8, 4, 4], P('fsdp', 'dp'), may hold values from 0 to 3, as said below
- ln_gain: float32 [1408], replicated, may hold values from 0.5 to 1.5
- ln_shift: float32 [1408], replicated, may hold values from -2.5 to 2.5
- w_qkv: bfloat16 [1408, 4224], P('fsdp')
- b_qkv: float32 [4224], replicated, may hold values from -2.5 to 2.5
- w_proj: bfloat16 [1408, 1408], P('fsdp'), may hold values from -0.15625 to 0.15625
- b_proj: float32 [1408], replicated, may hold values from -3 to 3
- grad_out: bfloat16 [8, 1536, 1408], P('fsdp', 'dp'), may hold values from -6 to 6
Outputs:
- y_owned: bfloat16 [8, 1536, 1408], P('fsdp', 'dp')
- grad_tokens: bfloat16 [8, 1536, 1408], P('fsdp', 'dp')
- grad_qkv: float32 [1408, 4224], P('fsdp')
- grad_proj: float32 [1408, 1408], P('fsdp')
- grad_gain: float32 [1408], replicated
- grad_shift: float32 [1408], replicated
- grad_qkv_bias: float32 [4224], replicated
- grad_proj_bias: float32 [1408], replicated
Inputs may be any that keep to these rules, and one draw needn't show every extreme that they name: The 4 images of each loader hold exactly 384 patches together; every dp group has an image of exactly 192 patches. Each loader sends exactly one image to each of the 4 owners of its dp group, so every owner receives exactly 384 patches.
All inputs are finite; a program needn't handle non-finite values.
Results may differ from a plain program's by a relative error of at most 0.024.
Values may be sent and summed in bfloat16 or wider, within the bound.
A program may use at most 192 MiB of HBM per device.

v0:
```python
from functools import partial

import jax
import jax.numpy as jnp
from jax import lax
from jax.sharding import PartitionSpec as P

HEADS = 16


NEG_FILL = -1e30
LN_EPS = 1e-06


def attention_layer(segments, owned_rows, ln_gain, ln_shift, w_qkv, b_qkv, w_proj, b_proj):
    row_count, model_width = owned_rows.shape
    head_size = model_width // HEADS
    inputs = owned_rows.astype(jnp.float32)
    centre = jnp.mean(inputs, axis=1, keepdims=True)
    spread = jnp.mean(jnp.square(inputs - centre), axis=1, keepdims=True)
    normed = ((inputs - centre) * lax.rsqrt(spread + LN_EPS) * ln_gain + ln_shift).astype(
        jnp.bfloat16
    )
    joined = (jnp.dot(normed, w_qkv, preferred_element_type=jnp.float32) + b_qkv).astype(
        jnp.bfloat16
    )
    queries = joined[:, :model_width].reshape(row_count, HEADS, head_size).astype(jnp.float32)
    keys_all = (
        joined[:, model_width : 2 * model_width]
        .reshape(row_count, HEADS, head_size)
        .astype(jnp.float32)
    )
    values_all = (
        joined[:, 2 * model_width :].reshape(row_count, HEADS, head_size).astype(jnp.float32)
    )
    scores = jnp.einsum("qhd,khd->hqk", queries, keys_all) * head_size ** (-0.5)
    same_image = segments[:, None] == segments[None, :]
    scores = jnp.where(same_image[None], scores, NEG_FILL)
    row_peak = lax.stop_gradient(jnp.max(scores, axis=2, keepdims=True))
    exp_scores = jnp.exp(scores - row_peak)
    attention_weights = (exp_scores / jnp.sum(exp_scores, axis=2, keepdims=True)).astype(
        jnp.bfloat16
    )
    context = jnp.einsum("hqk,khd->qhd", attention_weights.astype(jnp.float32), values_all)
    context = context.reshape(row_count, model_width).astype(jnp.bfloat16)
    layer_out = jnp.dot(context, w_proj, preferred_element_type=jnp.float32) + b_proj + inputs
    return layer_out.astype(jnp.bfloat16)


def pack_slots(data_rows, starts, counts, within):
    row_index = starts[:, None] + within[None, :]
    is_live = within[None, :] < counts[:, None]
    row_index = jnp.where(is_live, row_index, 0)
    return jnp.where(is_live[:, :, None], data_rows[row_index], jnp.zeros((), data_rows.dtype))


def regroup(pieces, dp_size, model_width):
    column_count = pieces.shape[2]
    stacked = pieces.reshape(dp_size, model_width, column_count)
    return jnp.transpose(stacked, (1, 0, 2)).reshape(model_width, dp_size * column_count)


def per_device(tokens, patches, owners, ln_gain, ln_shift, w_qkv, b_qkv, w_proj, b_proj, grad_out):
    loader_rows = tokens[0]
    row_count, model_width = loader_rows.shape
    dp_size = lax.axis_size("dp")
    fsdp_size = lax.axis_size("fsdp")
    my_index = lax.axis_index("dp")
    slot_rows = 2 * row_count // dp_size
    peer_ids = jnp.arange(dp_size, dtype=jnp.int32)
    within = jnp.arange(slot_rows, dtype=jnp.int32)
    positions = jnp.arange(row_count, dtype=jnp.int32)
    all_lengths, all_owners = (
        lax.all_gather(patches, "dp", axis=1, tiled=True),
        lax.all_gather(owners, "dp", axis=1, tiled=True),
    )
    all_lengths = all_lengths[0]
    all_owners = all_owners[0]
    owner_hits = (all_owners[:, :, None] == peer_ids[None, None, :]).astype(jnp.int32)
    pair_length = jnp.sum(all_lengths[:, :, None] * owner_hits, axis=1)
    pair_offset = jnp.cumsum(pair_length, axis=0) - pair_length
    my_lengths = patches[0, 0]
    my_targets = owners[0, 0]
    slot_start = jnp.cumsum(my_lengths) - my_lengths
    slot_end = slot_start + my_lengths
    to_peer = (my_targets[:, None] == peer_ids[None, :]).astype(jnp.int32)
    send_start = jnp.sum(to_peer * slot_start[:, None], axis=0)
    send_count = jnp.sum(to_peer * my_lengths[:, None], axis=0)
    outgoing = pack_slots(loader_rows, send_start, send_count, within)
    arrived = lax.all_to_all(outgoing, "dp", split_axis=0, concat_axis=0, tiled=True)
    from_count = pair_length[:, my_index]
    from_offset = pair_offset[:, my_index]
    source = jnp.sum(
        (positions[:, None] >= (from_offset + from_count)[None, :]).astype(jnp.int32), axis=1
    )
    source_hit = (source[:, None] == peer_ids[None, :]).astype(jnp.int32)
    place_in = positions - jnp.sum(source_hit * from_offset[None, :], axis=1)
    owned_rows = arrived.reshape(dp_size * slot_rows, model_width)[source * slot_rows + place_in]
    qkv_columns = w_qkv.shape[1] // dp_size
    proj_columns = w_proj.shape[1] // dp_size
    part_qkv = lax.dynamic_slice_in_dim(w_qkv, my_index * qkv_columns, qkv_columns, 1)[None]
    part_proj = lax.dynamic_slice_in_dim(w_proj, my_index * proj_columns, proj_columns, 1)[None]
    got_qkv, got_proj = (
        lax.all_gather(part_qkv, ("dp", "fsdp"), axis=0, tiled=True),
        lax.all_gather(part_proj, ("dp", "fsdp"), axis=0, tiled=True),
    )
    full_qkv = regroup(got_qkv, dp_size, model_width)
    full_proj = regroup(got_proj, dp_size, model_width)
    layer_out, backward = jax.vjp(
        partial(attention_layer, source),
        owned_rows,
        ln_gain,
        ln_shift,
        full_qkv,
        b_qkv,
        full_proj,
        b_proj,
    )
    gradients = backward(grad_out[0])
    returning = pack_slots(gradients[0], from_offset, from_count, within)
    returned = lax.all_to_all(returning, "dp", split_axis=0, concat_axis=0, tiled=True)
    slot_of_row = jnp.sum((positions[:, None] >= slot_end[None, :]).astype(jnp.int32), axis=1)
    slot_hit = (slot_of_row[:, None] == peer_ids[None, :]).astype(jnp.int32)
    row_owner = jnp.sum(slot_hit * my_targets[None, :], axis=1)
    row_place = positions - jnp.sum(slot_hit * slot_start[None, :], axis=1)
    grad_rows = returned.reshape(dp_size * slot_rows, model_width)[
        row_owner * slot_rows + row_place
    ]
    shard_qkv, shard_proj = (
        lax.psum_scatter(
            gradients[3].astype(jnp.float32).astype(jnp.bfloat16),
            "fsdp",
            scatter_dimension=0,
            tiled=True,
        ).astype(jnp.float32),
        lax.psum_scatter(
            gradients[5].astype(jnp.float32).astype(jnp.bfloat16),
            "fsdp",
            scatter_dimension=0,
            tiled=True,
        ).astype(jnp.float32),
    )
    summed_qkv, summed_proj = (
        lax.psum(shard_qkv.astype(jnp.bfloat16), "dp").astype(jnp.float32),
        lax.psum(shard_proj.astype(jnp.bfloat16), "dp").astype(jnp.float32),
    )
    small_sums = lax.psum((gradients[1], gradients[2], gradients[4], gradients[6]), ("dp", "fsdp"))
    device_share = 1.0 / (dp_size * fsdp_size)
    return (
        layer_out[None],
        grad_rows[None],
        summed_qkv * device_share,
        summed_proj * device_share,
        small_sums[0] * device_share,
        small_sums[1] * device_share,
        small_sums[2] * device_share,
        small_sums[3] * device_share,
    )


def solution(mesh):
    placed = (
        P("fsdp", "dp", None),
        P("fsdp", "dp", None),
        P("fsdp", "dp", None),
        P(),
        P(),
        P("fsdp", None),
        P(),
        P("fsdp", None),
        P(),
        P("fsdp", "dp", None),
    )
    return jax.shard_map(
        per_device,
        mesh=mesh,
        in_specs=placed,
        out_specs=(
            P("fsdp", "dp", None),
            P("fsdp", "dp", None),
            P("fsdp", None),
            P("fsdp", None),
            P(),
            P(),
            P(),
            P(),
        ),
        check_vma=False,
    )
```

profile of v0, /device:TPU:0, one launch (start us, length us, event | category | flops | bytes accessed | tf_op | source)
XLA Modules:
  0.0 602.7 jit_solution(3291951950299038871)
XLA Ops:
  12.6 3.7 gather_fusion
  16.4 3.2 broadcast_select_fusion.1
  19.6 4.4 all-to-all-start
  24.0 29.2 %all_gather.13 = s32[1,4,4]{2,0,1:T(1,128)S(1)} all-gather(s32[1,1,4]{2,0,1:T(1,128)S(1)} %bitcast.113), channel_id=1, replica_groups=mesh['dp'=4,'fsdp'=8] {'dp'}, dimensions={1}, use_global_device_ids=true | all-gather | bytes 80 | tf_op jit(solution)/shard_map/all_gather | solution.py:74
  53.2 5.0 all_gather.12
  62.0 15.6 %all-gather.7.cloned.1.call-done = bf16[5632,352]{1,0:T(8,128)(2,1)} async-done(((bf16[176,352]{1,0:T(8,128)(2,1)}), bf16[5632,352]{1,0:T(8,128)(2,1)}) %all-gather.7.cloned.1.call-update) | async-done | bytes 3964944 | tf_op jit(solution)/shard_map/all_gather | solution.py:105
  77.6 8.7 %copy.90 = bf16[4,1408,352]{1,0,2:T(4,128)(2,1)} copy(bf16[4,1408,352]{2,1,0:T(8,128)(2,1)} %bitcast.83) | data formatting | bytes 7929856 | tf_op jit(solution)/shard_map/reshape | solution.py:59
  86.3 2.9 copy.81
  91.1 3.4 convolution_convert_fusion.3
  94.4 82.9 %all-gather.5.cloned.1.call-done = bf16[5632,1056]{1,0:T(8,128)(2,1)} async-done(((bf16[176,1056]{1,0:T(8,128)(2,1)}), bf16[5632,1056]{1,0:T(8,128)(2,1)}) %all-gather.5.cloned.1.call-update) | async-done | bytes 11894800 | tf_op jit(solution)/shard_map/all_gather | solution.py:104
  177.4 23.7 %copy.89 = bf16[4,1408,1056]{1,0,2:T(4,128)(2,1)} copy(bf16[4,1408,1056]{2,1,0:T(8,128)(2,1)} %bitcast.78) | data formatting | bytes 23789568 | tf_op jit(solution)/shard_map/reshape | solution.py:59
  201.1 11.5 %copy.75 = bf16[1408,4,1056]{0,2,1:T(8,128)(2,1)} copy(bf16[1408,4,1056]{0,1,2:T(4,128)(2,1)} %bitcast.76) | data formatting | bytes 23789568 | tf_op jit(solution)/shard_map/transpose | solution.py:60
  212.6 12.4 %fusion.8 = bf16[384,4224]{1,0:T(8,128)(2,1)S(1)} fusion(bf16[1408,4224]{0,1:T(8,128)(2,1)} %bitcast.79, f32[4224]{0:T(1024)S(1)} %copy-done.19, bf16[384,1408]{1,0:T(8,128)(2,1)S(1)} %gather_fusion.1, f32[1408]{0:T(1024)S(1)} %copy-done.20, f32[1408]{0:T(1024)S(1)} %copy-done.16, f32[384]{0:T(512)S(1)} %fusion.34, f32[384]{0:T(512)S(1)} %broadcast_multiply_fusion.4), kind=kOutput, calls=%fused_computation.20 | convolution fusion | flops 4574085120 | bytes 16251392 | tf_op jit(solution)/shard_map/jvp()/dot_general | solution.py:24
  226.2 2.3 copy.77
  230.3 8.3 %fusion.44 = (f32[16,384]{1,0:T(8,128)S(1)}, f32[16,384,384]{1,2,0:T(8,128)}) fusion(pred[384,384]{0,1:T(8,128)(4,1)S(1)} %broadcast_compare_fusion, bf16[384,16,88]{0,2,1:T(8,128)(2,1)} %bitcast.97, bf16[384,16,88]{0,2,1:T(8,128)(2,1)} %bitcast.99), kind=kOutput, calls=%fused_computation.116 | convolution fusion | flops 424673664 | bytes 11771904 | tf_op jit(solution)/shard_map/jvp()/sub | solution.py:40
  240.0 8.2 %fusion.6 = (f32[16,384]{1,0:T(8,128)S(1)}, bf16[16,384,384]{1,2,0:T(8,128)(2,1)S(1)}, bf16[16,384,384]{1,2,0:T(8,128)(2,1)}) fusion(f32[16,384,384]{1,2,0:T(8,128)} %get-tuple-element.30, f32[16,384]{1,0:T(8,128)S(1)} %multiply_divide_fusion, f32[16,384]{1,0:T(8,128)S(1)} %get-tuple-element.29, bf16[16,88,384]{2,1,0:T(8,128)(2,1)} %bitcast.103, ...), kind=kOutput, calls=%fused_computation.13 | convolution fusion | flops 431745024 | bytes 21110784 | tf_op jit(solution)/shard_map/transpose(jvp(hqk,khd->qhd))/dot_general | solution.py:44
  252.5 4.3 convolution_convert_fusion.1
  258.1 4.4 convolution_convert_fusion.7
  262.6 7.0 %convolution_convert_fusion.5 = bf16[16,384,88]{1,2,0:T(8,128)(2,1)S(1)} fusion(bf16[384,16,88]{0,2,1:T(8,128)(2,1)S(1)} %bitcast.100, f32[16,384,384]{1,2,0:T(8,128)} %get-tuple-element.30, bf16[16,384,384]{1,2,0:T(8,128)(2,1)S(1)} %copy-done.22, f32[16,384]{1,0:T(8,128)S(1)} %neg.12, f32[16,384]{1,0:T(8,128)S(1)} %get-tuple-element.29, ...), kind=kOutput, calls=%fused_computation.59 | convolution fusion | flops 429932544 | bytes 16515072 | tf_op jit(solution)/shard_map/transpose(jvp(qhd,khd->hqk))/dot_general | solution.py:36
  269.6 8.4 %convolution_convert_fusion.6 = bf16[16,384,88]{1,2,0:T(8,128)(2,1)S(1)} fusion(bf16[384,16,88]{0,2,1:T(8,128)(2,1)S(1)} %bitcast.98, f32[16,384,384]{1,2,0:T(8,128)} %get-tuple-element.30, bf16[16,384,384]{1,2,0:T(8,128)(2,1)} %get-tuple-element.31, f32[16,384]{1,0:T(8,128)S(1)} %neg.12, f32[16,384]{1,0:T(8,128)S(1)} %get-tuple-element.29, ...), kind=kOutput, calls=%fused_computation.60 | convolution fusion | flops 429932544 | bytes 16515072 | tf_op jit(solution)/shard_map/transpose(jvp(qhd,khd->hqk))/dot_general | solution.py:36
  278.9 12.8 %convolution_convert_fusion = bf16[1408,4224]{1,0:T(8,128)(2,1)} fusion(bf16[384,1408]{1,0:T(8,128)(2,1)S(1)} %gather_fusion.1, f32[1408]{0:T(1024)S(1)} %copy-done.20, f32[1408]{0:T(1024)S(1)} %copy-done.16, f32[384]{0:T(512)S(1)} %fusion.34, f32[384]{0:T(512)S(1)} %broadcast_multiply_fusion.4, bf16[384,1408]{0,1:T(8,128)(2,1)S(1)} %bitcast.91, ...), kind=kOutput, calls=%fused_computation.5 | convolution fusion | flops 4586520576 | bytes 16234496 | tf_op jit(solution)/shard_map/transpose(jvp())/dot_general | solution.py:24
  292.2 11.0 %fusion.29 = (f32[1408]{0:T(1024)S(1)}, f32[384]{0:T(512)S(1)}, f32[384]{0:T(512)S(1)}, f32[1408]{0:T(1024)S(1)}, bf16[384,1408]{1,0:T(8,128)(2,1)S(1)}) fusion(bf16[384,1408]{1,0:T(8,128)(2,1)S(1)} %gather_fusion.1, f32[384]{0:T(512)S(1)} %fusion.34, f32[384]{0:T(512)S(1)} %broadcast_multiply_fusion.4, f32[1408]{0:T(1024)S(1)} %copy-done.16, ...), kind=kOutput, calls=%fused_computation.56 | convolution fusion | flops 4584353792 | bytes 17324544 | tf_op jit(solution)/shard_map/transpose(jvp())/dot_general | solution.py:24
  304.6 3.8 gather_fusion.2
  308.4 3.2 broadcast_select_fusion
  311.6 3.6 all-to-all-start.1
  315.3 2.5 convert_reduce_fusion
  317.9 61.1 %all-reduce.3 = (f32[1408]{0:T(1024)S(1)}, f32[1408]{0:T(1024)S(1)}, f32[4224]{0:T(1024)S(1)}, f32[1408]{0:T(1024)S(1)}) all-reduce(f32[1408]{0:T(1024)S(1)} %get-tuple-element.8, f32[1408]{0:T(1024)S(1)} %get-tuple-element.11, f32[4224]{0:T(1024)S(1)} %convert_reduce_fusion, ...), channel_id=1, replica_groups=mesh['dp'=4,'fsdp'=8] {'dp','fsdp'}, use_global_device_ids=true, to_apply=%region_23.24 | all-reduce | flops 8448 | bytes 67584 | tf_op jit(solution)/shard_map/psum | solution.py:147
  380.1 160.1 %reduce-scatter.3.cloned.1.call-done = bf16[176,4224]{1,0:T(8,128)(2,1)} async-done(((bf16[1408,4224]{1,0:T(8,128)(2,1)}), bf16[176,4224]{1,0:T(8,128)(2,1)}) %reduce-scatter.3.cloned.1.call-update) | async-done | bytes 1486864 | tf_op jit(solution)/shard_map/reduce_scatter | solution.py:130
  541.5 5.5 fusion.17
  546.9 2.8 gather_fusion.3
  549.7 41.9 %all-reduce.7.cloned.1.call-done = (bf16[176,4224]{1,0:T(8,128)(2,1)}, bf16[176,1408]{1,0:T(8,128)(2,1)}) async-done(((bf16[176,4224]{1,0:T(8,128)(2,1)}, bf16[176,1408]{1,0:T(8,128)(2,1)}), (bf16[176,4224]{1,0:T(8,128)(2,1)}, bf16[176,1408]{1,0:T(8,128)(2,1)})) %all-reduce.7.cloned.1.call-update) | async-done | bytes 1982480 | tf_op jit(solution)/shard_map/psum | solution.py:144
  591.6 3.3 convert_multiply_fusion.3
  (108 shorter events, 27.1 us)
Async XLA Ops:
  7.2 2.0 copy-start
  7.2 5.4 copy-start.2
  7.2 70.4 %all-gather.7.cloned.1.call-start = ((), (), s32[]{:S(2)}) async-start(), calls=%async_computation.7 | async-start | bytes 4460544 | tf_op jit(solution)/shard_map/all_gather | solution.py:105
  9.1 168.3 %all-gather.5.cloned.1.call-start = ((), (), s32[]{:S(2)}) async-start(), calls=%async_computation.6 | async-start | bytes 13381632 | tf_op jit(solution)/shard_map/all_gather | solution.py:104
  19.6 4.4 copy-start.18
  19.6 33.6 %copy-start.17 = (s32[1,1,4]{2,1,0:T(1,128)S(1)}, s32[1,1,4]{2,1,0:T(1,128)}, u32[]{:S(2)}) copy-start(s32[1,1,4]{2,1,0:T(1,128)} %param.12) | copy-start | bytes 52
  19.6 39.4 %all-to-all-start = ((bf16[4,192,1408]{2,1,0:T(8,128)(2,1)}), bf16[4,192,1408]{2,1,0:T(8,128)(2,1)S(1)}, u32[]{:S(2)}, u32[]{:S(2)}) async-start(bf16[4,192,1408]{2,1,0:T(8,128)(2,1)} %broadcast_select_fusion.1), calls=%async_computation | async-start | bytes 4325376 | tf_op jit(solution)/shard_map/all_to_all | solution.py:90
  24.0 356.1 %reduce-scatter.5.cloned.1.call-start = ((), (), s32[]{:S(2)}) async-start(), calls=%async_computation.5 | async-start | bytes 4460544 | tf_op jit(solution)/shard_map/reduce_scatter | solution.py:136
  86.3 4.8 copy-start.10
  89.2 1.9 copy-start.5
  201.1 11.5 %copy-start.16 = (f32[1408]{0:T(1024)S(1)}, f32[1408]{0:T(1024)}, u32[]{:S(2)}) copy-start(f32[1408]{0:T(1024)} %param.13) | copy-start | bytes 16900
  201.1 11.5 %copy-start.19 = (f32[4224]{0:T(1024)S(1)}, f32[4224]{0:T(1024)}, u32[]{:S(2)}) copy-start(f32[4224]{0:T(1024)} %param.16) | copy-start | bytes 50692
  201.1 11.5 %copy-start.20 = (f32[1408]{0:T(1024)S(1)}, f32[1408]{0:T(1024)}, u32[]{:S(2)}) copy-start(f32[1408]{0:T(1024)} %param.14) | copy-start | bytes 16900
  248.2 2.3 copy-start.3
  250.5 2.1 copy-start.11
  251.6 1.0 copy-start.13
  256.9 1.2 copy-start.14
  256.9 283.3 %reduce-scatter.3.cloned.1.call-start = ((), (), s32[]{:S(2)}) async-start(), calls=%async_computation.4 | async-start | bytes 13381632 | tf_op jit(solution)/shard_map/reduce_scatter | solution.py:130
  258.1 4.5 copy-start.9
  258.1 4.5 copy-start.22
  262.6 29.7 %copy-start.4 = (bf16[16,88,384]{2,1,0:T(8,128)(2,1)}, bf16[16,88,384]{2,1,0:T(8,128)(2,1)S(1)}, u32[]{:S(2)}) copy-start(bf16[16,88,384]{2,1,0:T(8,128)(2,1)S(1)} %convolution_convert_fusion.7) | copy-start | bytes 3244036
  262.6 7.0 %copy-start.8 = (bf16[384,1408]{0,1:T(8,128)(2,1)S(1)}, bf16[384,1408]{0,1:T(8,128)(2,1)}, u32[]{:S(2)}) copy-start(bf16[384,1408]{0,1:T(8,128)(2,1)} %copy.77) | copy-start | bytes 3244036
  269.6 22.7 %copy-start.6 = (bf16[16,384,88]{1,2,0:T(8,128)(2,1)}, bf16[16,384,88]{1,2,0:T(8,128)(2,1)S(1)}, u32[]{:S(2)}) copy-start(bf16[16,384,88]{1,2,0:T(8,128)(2,1)S(1)} %convolution_convert_fusion.5) | copy-start | bytes 3244036
  277.9 1.0 copy-start.7
  292.2 11.5 %copy-start.12 = (bf16[1,384,1408]{2,1,0:T(8,128)(2,1)S(1)}, bf16[1,384,1408]{2,1,0:T(8,128)(2,1)}, u32[]{:S(2)}) copy-start(bf16[1,384,1408]{2,1,0:T(8,128)(2,1)} %param.19) | copy-start | bytes 3244036
  311.6 235.3 %all-to-all-start.1 = ((bf16[4,192,1408]{2,1,0:T(8,128)(2,1)}), bf16[4,192,1408]{2,1,0:T(8,128)(2,1)S(1)}, u32[]{:S(2)}, u32[]{:S(2)}) async-start(bf16[4,192,1408]{2,1,0:T(8,128)(2,1)} %broadcast_select_fusion), calls=%async_computation.1 | async-start | bytes 4325376 | tf_op jit(solution)/shard_map/all_to_all | solution.py:121
  315.3 226.2 %copy-start.21 = (f32[1408]{0:T(1024)S(1)}, f32[1408]{0:T(1024)}, u32[]{:S(2)}) copy-start(f32[1408]{0:T(1024)} %param.18) | copy-start | bytes 16900
  315.3 276.3 %all-reduce.7.cloned.1.call-start = ((), (), s32[]{:S(2)}) async-start(), calls=%async_computation.8 | async-start | bytes 3964928 | tf_op jit(solution)/shard_map/psum | solution.py:144
  591.6 4.3 copy-start.1
  591.6 3.3 copy-start.15
Sparse Core Ops, SparseCore 0:
  11.6 65.9 all-gather.6
  81.2 96.1 all-gather.4
  257.0 81.7 reduce-scatter.4
  342.3 197.9 reduce-scatter.2
  542.5 48.9 all-reduce.6
where the time goes:
time: 613 us; the launch traced here: 603 us
  waiting for transfers between devices  301 us (49%)
  blocking collectives  95.3 us (16%)
  matrix products  86.8 us (14%)
  local copies, waits for them, and re-layouts  76.4 us (12%)
  other arithmetic  21.1 us (3%)
  between operations  14.3 us (2%)
  starting transfers between devices  8.15 us (1%)
    reduce_scatter x1, waiting for transfers between devices, per_device(): lax.psum_scatter(gradients[3].astype(jnp.float32).astype(jnp.bfloat16), '...  160 us
    all_gather x1, waiting for transfers between devices, per_device(): lax.all_gather(part_qkv, ('dp', 'fsdp'), axis=0, tiled=True)  82.9 us
    psum x1, blocking collectives, per_device(): lax.psum((gradients[1], gradients[2], gradients[4], gradients[6]), ('dp',...  61.1 us
    psum x1, waiting for transfers between devices, per_device(): lax.psum(shard_qkv.astype(jnp.bfloat16), 'dp').astype(jnp.float32)  41.9 us
    dot_general x3, matrix products, attention_layer(): jnp.dot(normed, w_qkv, preferred_element_type=jnp.float32) + b_qkv  36.2 us
    reshape x2, local copies, waits for them, and re-layouts, regroup(): stacked = pieces.reshape(dp_size, model_width, column_count)  32.4 us
    all_gather x1, blocking collectives, per_device(): lax.all_gather(patches, 'dp', axis=1, tiled=True)  29.2 us
    all_gather x1, waiting for transfers between devices, per_device(): lax.all_gather(part_proj, ('dp', 'fsdp'), axis=0, tiled=True)  15.6 us
  transfers between devices with their start and end apart: 7, of which 4 were waited for; matrix products, arithmetic and copies ran while one was open for 16% of the time, Pallas kernels for 0%

commit v1 on v0

v1 whole, which is shorter than its diff:
```python
from functools import partial

import jax
import jax.numpy as jnp
from jax import lax
from jax.sharding import PartitionSpec as P

HEADS = 16


NEG_FILL = -1e30
LN_EPS = 1e-06


def layer_norm(rows, ln_gain, ln_shift):
    inputs = rows.astype(jnp.float32)
    centre = jnp.mean(inputs, axis=1, keepdims=True)
    spread = jnp.mean(jnp.square(inputs - centre), axis=1, keepdims=True)
    normed = ((inputs - centre) * lax.rsqrt(spread + LN_EPS) * ln_gain + ln_shift).astype(
        jnp.bfloat16
    )
    return normed, inputs


def attend(same_image, head_count, joined):
    loaders, row_count, _ = same_image.shape
    width = joined.shape[1] // 3
    head_size = width // head_count

    def heads_of(part):
        return part.reshape(loaders, row_count, head_count, head_size).astype(jnp.float32)

    queries = heads_of(joined[:, :width])
    keys = heads_of(joined[:, width : 2 * width])
    values = heads_of(joined[:, 2 * width :])
    scores = jnp.einsum("aqhd,akhd->ahqk", queries, keys) * head_size ** (-0.5)
    scores = jnp.where(same_image[:, None], scores, NEG_FILL)
    row_peak = lax.stop_gradient(jnp.max(scores, axis=3, keepdims=True))
    exp_scores = jnp.exp(scores - row_peak)
    weights = (exp_scores / jnp.sum(exp_scores, axis=3, keepdims=True)).astype(jnp.bfloat16)
    context = jnp.einsum("ahqk,akhd->aqhd", weights.astype(jnp.float32), values)
    return context.reshape(loaders * row_count, width).astype(jnp.bfloat16)


def per_device(tokens, patches, owners, ln_gain, ln_shift, w_qkv, b_qkv, w_proj, b_proj, grad_out):
    own_tokens = tokens[0]
    row_count, model_width = own_tokens.shape
    dp_size = lax.axis_size("dp")
    fsdp_size = lax.axis_size("fsdp")
    me = lax.axis_index("dp")
    shard = lax.axis_index("fsdp")
    head_count = HEADS // dp_size
    width = model_width // dp_size
    shard_rows = w_qkv.shape[0]

    w_part = jnp.concatenate(
        [
            lax.dynamic_slice_in_dim(w_qkv, part * model_width + me * width, width, 1)
            for part in range(3)
        ],
        axis=1,
    )
    b_part = lax.dynamic_slice_in_dim(b_qkv.reshape(3, dp_size, width), me, 1, axis=1).reshape(-1)

    all_tokens = lax.all_gather(own_tokens, "dp", axis=0, tiled=True)
    w_heads = lax.all_gather(w_part, "fsdp", axis=0, tiled=True)
    all_grad = lax.all_gather(grad_out[0], "dp", axis=0, tiled=True)
    w_full = lax.all_gather(w_proj, "fsdp", axis=0, tiled=True)
    tables = lax.all_gather(
        jnp.concatenate([patches, owners], axis=2), "dp", axis=1, tiled=True
    )[0]
    lengths, targets = tables[:, :dp_size], tables[:, dp_size:]

    positions = jnp.arange(row_count, dtype=jnp.int32)
    peers = jnp.arange(dp_size, dtype=jnp.int32)
    slot_start = jnp.cumsum(lengths, axis=1) - lengths
    slot_end = slot_start + lengths
    hits = (targets[:, :, None] == peers).astype(jnp.int32)
    pair_length = jnp.sum(lengths[:, :, None] * hits, axis=1)
    pair_start = jnp.sum(slot_start[:, :, None] * hits, axis=1)
    pair_offset = jnp.cumsum(pair_length, axis=0) - pair_length
    slot_base = (
        targets * row_count + jnp.sum(hits * pair_offset[:, None, :], axis=2) - slot_start
    )
    image = jnp.sum((positions[None, :, None] >= slot_end[:, None, :]).astype(jnp.int32), axis=2)
    image_hit = (image[:, :, None] == peers).astype(jnp.int32)
    destination = (
        jnp.sum(image_hit * slot_base[:, None, :], axis=2) + positions[None, :]
    ).reshape(-1)
    same_image = image[:, :, None] == image[:, None, :]
    pair_end = pair_offset + pair_length
    source = jnp.sum(
        (positions[None, :, None] >= pair_end.T[:, None, :]).astype(jnp.int32), axis=2
    )
    source_hit = (source[:, :, None] == peers).astype(jnp.int32)
    pair_base = (peers[:, None] * row_count + pair_start - pair_offset).T
    origin = jnp.sum(source_hit * pair_base[:, None, :], axis=2) + positions[None, :]

    normed, _ = layer_norm(all_tokens, ln_gain, ln_shift)
    joined = (jnp.dot(normed, w_heads, preferred_element_type=jnp.float32) + b_part).astype(
        jnp.bfloat16
    )
    context, attend_back = jax.vjp(partial(attend, same_image, head_count), joined)
    grad_rows = all_grad[destination]
    w_rows = lax.dynamic_slice_in_dim(w_full, me * width, width, 0)
    grad_context = lax.dot_general(
        grad_rows, w_rows, (((1,), (1,)), ((), ())), preferred_element_type=jnp.float32
    ).astype(jnp.bfloat16)
    (grad_joined,) = attend_back(grad_context)

    term_proj = lax.dot_general(
        context, grad_rows, (((0,), (0,)), ((), ())), preferred_element_type=jnp.float32
    ).astype(jnp.bfloat16)
    rows_proj = lax.psum(term_proj, "fsdp")
    per_block = width // shard_rows
    mine = lax.dynamic_slice_in_dim(rows_proj, (shard % per_block) * shard_rows, shard_rows, 0)
    mine = jnp.where(shard // per_block == me, mine, jnp.zeros((), mine.dtype))
    summed_proj = lax.psum(mine, "dp")

    term_qkv = lax.dot_general(
        normed, grad_joined, (((0,), (0,)), ((), ())), preferred_element_type=jnp.float32
    ).astype(jnp.bfloat16)
    shard_qkv = lax.psum_scatter(term_qkv, "fsdp", scatter_dimension=0, tiled=True)
    all_qkv = lax.all_gather(shard_qkv, "dp", axis=0)
    summed_qkv = jnp.concatenate(
        [
            all_qkv[peer, :, part * width : (part + 1) * width]
            for part in range(3)
            for peer in range(dp_size)
        ],
        axis=1,
    )

    part_normed = lax.dot_general(
        grad_joined, w_heads, (((1,), (1,)), ((), ())), preferred_element_type=jnp.float32
    ).astype(jnp.bfloat16)
    parts = lax.all_to_all(
        part_normed.reshape(dp_size, row_count, model_width), "dp", 0, 0, tiled=True
    )
    grad_normed = jnp.sum(parts.astype(jnp.float32), axis=0).astype(jnp.bfloat16)
    own_grad = lax.dynamic_slice_in_dim(grad_rows, me * row_count, row_count, 0).astype(
        jnp.float32
    )
    _, norm_back = jax.vjp(layer_norm, own_tokens, ln_gain, ln_shift)
    grad_tokens, gain_term, shift_term = norm_back((grad_normed, own_grad))

    context_out = lax.all_to_all(
        context[origin.reshape(-1)].reshape(dp_size, row_count, width), "dp", 0, 0, tiled=True
    )
    own_context = jnp.concatenate([context_out[peer] for peer in range(dp_size)], axis=1)
    own_origin = lax.dynamic_slice_in_dim(origin, me, 1, 0)[0]
    owned = all_tokens[own_origin].astype(jnp.float32)
    y_owned = (
        jnp.dot(own_context, w_full, preferred_element_type=jnp.float32) + b_proj + owned
    ).astype(jnp.bfloat16)

    bias_part = jnp.sum(grad_joined.astype(jnp.float32), axis=0).reshape(3, 1, width)
    bias_term = jnp.where(
        peers[None, :, None] == me, bias_part, jnp.zeros((), jnp.float32)
    ).reshape(-1)
    proj_term = jnp.sum(grad_out[0].astype(jnp.float32), axis=0)
    small = lax.all_gather(
        jnp.concatenate([gain_term, shift_term, bias_term, proj_term]), ("dp", "fsdp")
    )
    device_share = 1.0 / (dp_size * fsdp_size)
    small = jnp.sum(small, axis=0) * device_share
    cuts = (model_width, 2 * model_width, 5 * model_width)
    gain, shift, qkv_bias, proj_bias = jnp.split(small, cuts)
    return (
        y_owned[None],
        grad_tokens[None],
        summed_qkv.astype(jnp.float32) * device_share,
        summed_proj.astype(jnp.float32) * device_share,
        gain,
        shift,
        qkv_bias,
        proj_bias,
    )


def solution(mesh):
    placed = (
        P("fsdp", "dp", None),
        P("fsdp", "dp", None),
        P("fsdp", "dp", None),
        P(),
        P(),
        P("fsdp", None),
        P(),
        P("fsdp", None),
        P(),
        P("fsdp", "dp", None),
    )
    return jax.shard_map(
        per_device,
        mesh=mesh,
        in_specs=placed,
        out_specs=(
            P("fsdp", "dp", None),
            P("fsdp", "dp", None),
            P("fsdp", None),
            P("fsdp", None),
            P(),
            P(),
            P(),
            P(),
        ),
        check_vma=False,
    )
```

time: 613 us -> 546 us (0.89); the launches traced: 603 us -> 542 us
  blocking collectives: 95.3 us -> 5.97 us
  waiting for transfers between devices: 301 us -> 359 us
  local copies, waits for them, and re-layouts: 76.4 us -> 47.2 us
  matrix products: 86.8 us -> 75.2 us
  other arithmetic: 21.1 us -> 30.6 us
    all_gather x2 -> x6, waiting for transfers between devices: 98.6 us -> 231 us  [the longest x1 59.6 us: per_device(): w_heads = lax.all_gather(w_part, 'fsdp', axis=0, tiled=True)]
    reduce_scatter x2 -> x1, waiting for transfers between devices: 160 us -> 36.3 us  [per_device(): lax.psum_scatter(term_qkv, 'fsdp', scatter_dimension=0, tiled=True)]
    psum x1 -> x0, blocking collectives: 61.1 us -> none  [per_device(): lax.psum((gradients[1], gradients[2], gradients[4], gradients[6]), ('dp',...]
    psum x1 -> x2, waiting for transfers between devices: 41.9 us -> 82.2 us  [the longest x1 47.3 us: per_device(): rows_proj = lax.psum(term_proj, 'fsdp')]
    all_gather x2 -> x1, blocking collectives: 34.2 us -> 5.97 us  [per_device(): lax.all_gather(jnp.concatenate([patches, owners], axis=2), 'dp', axis=1,...]
    reshape x2 -> x6, local copies, waits for them, and re-layouts: 32.4 us -> 6.26 us  [the longest x3 2.49 us: heads_of(): part.reshape(loaders, row_count, head_count, head_size).astype(jnp.float32)]
    transpose x2 -> x1, local copies, waits for them, and re-layouts: 14.4 us -> 0.09 us  [per_device(): pair_end.T[:, None, :]]
    gather x4 -> x3, local copies, waits for them, and re-layouts: 12.6 us -> 24.4 us  [the longest x1 12.3 us: per_device(): grad_rows = all_grad[destination]]
  transfers between devices with their start and end apart: 7 -> 11, of which waited for: 4 -> 10; matrix products, arithmetic and copies ran while one was open for 16% -> 19% of each run, Pallas kernels for 0% -> 0%
where the time goes in v1:
time: 546 us; the launch traced here: 542 us
  waiting for transfers between devices  359 us (66%)
  matrix products  75.2 us (14%)
  local copies, waits for them, and re-layouts  47.2 us (9%)
  other arithmetic  30.6 us (6%)
  between operations  14.8 us (3%)
  starting transfers between devices  9.12 us (2%)
  blocking collectives  5.97 us (1%)
    all_gather x1, waiting for transfers between devices, per_device(): w_heads = lax.all_gather(w_part, 'fsdp', axis=0, tiled=True)  59.6 us
    all_gather x1, waiting for transfers between devices, per_device(): w_full = lax.all_gather(w_proj, 'fsdp', axis=0, tiled=True)  51.9 us
    all_gather x1, waiting for transfers between devices, per_device(): lax.all_gather(jnp.concatenate([gain_term, shift_term, bias_term, proj_te...  51.6 us
    psum x1, waiting for transfers between devices, per_device(): rows_proj = lax.psum(term_proj, 'fsdp')  47.3 us
    reduce_scatter x1, waiting for transfers between devices, per_device(): lax.psum_scatter(term_qkv, 'fsdp', scatter_dimension=0, tiled=True)  36.3 us
    psum x1, waiting for transfers between devices, per_device(): summed_proj = lax.psum(mine, 'dp')  34.9 us
    all_gather x1, waiting for transfers between devices, per_device(): all_tokens = lax.all_gather(own_tokens, 'dp', axis=0, tiled=True)  27.4 us
    all_gather x1, waiting for transfers between devices, per_device(): all_grad = lax.all_gather(grad_out[0], 'dp', axis=0, tiled=True)  23.1 us
  transfers between devices with their start and end apart: 11, of which 10 were waited for; matrix products, arithmetic and copies ran while one was open for 19% of the time, Pallas kernels for 0%

profile of v1, /device:TPU:0, one launch (start us, length us, event | category | flops | bytes accessed | tf_op | source)
XLA Modules:
  0.0 542.2 jit_solution(9321845352662643018)
XLA Ops:
  11.8 6.0 %all_gather.29 = s32[1,4,8]{2,0,1:T(1,128)S(1)} all-gather(s32[1,1,8]{2,0,1:T(1,128)S(1)} %pad_add_fusion.1), channel_id=1, replica_groups=mesh['dp'=4,'fsdp'=8] {'dp'}, dimensions={1}, use_global_device_ids=true | all-gather | bytes 160 | tf_op jit(solution)/shard_map/all_gather | solution.py:69
  20.1 27.4 %all-gather.16.cloned.1.call-done = bf16[1,1536,1408]{2,1,0:T(8,128)(2,1)} async-done(((bf16[1,384,1408]{2,1,0:T(8,128)(2,1)}), bf16[1,1536,1408]{2,1,0:T(8,128)(2,1)}) %all-gather.16.cloned.1.call-update) | async-done | bytes 4325392 | tf_op jit(solution)/shard_map/all_gather | solution.py:65
  47.6 3.0 convert_reduce_fusion
  52.4 59.6 %all-gather.12.cloned.1.call-done = bf16[1408,1056]{1,0:T(8,128)(2,1)} async-done(((bf16[176,1056]{1,0:T(8,128)(2,1)}), bf16[1408,1056]{1,0:T(8,128)(2,1)}) %all-gather.12.cloned.1.call-update) | async-done | bytes 2973712 | tf_op jit(solution)/shard_map/all_gather | solution.py:66
  111.9 9.6 %fusion.13 = bf16[1536,1056]{0,1:T(8,128)(2,1)S(1)} fusion(bf16[1408,1056]{1,0:T(8,128)(2,1)} %all-gather.12.cloned.1.call-done, f32[1056]{0:T(1024)S(1)} %add.194, f32[1408]{0:T(1024)S(1)} %copy-done.10, f32[1408]{0:T(1024)S(1)} %copy-done.8, f32[1536]{0:T(1024)S(1)} %add_rsqrt_fusion, f32[1536]{0:T(1024)S(1)} %broadcast_multiply_fusion.1, ...), kind=kOutput, calls=%fused_computation.24 | convolution fusion | flops 4583817216 | bytes 10570880 | tf_op jit(solution)/shard_map/dot_general | solution.py:100
  124.3 23.1 %all-gather.18.cloned.1.call-done = bf16[1,1536,1408]{2,1,0:T(8,128)(2,1)} async-done(((bf16[1,384,1408]{2,1,0:T(8,128)(2,1)}), bf16[1,1536,1408]{2,1,0:T(8,128)(2,1)}) %all-gather.18.cloned.1.call-update) | async-done | bytes 4325392 | tf_op jit(solution)/shard_map/all_gather | solution.py:67
  147.4 12.3 %gather_fusion.2 = bf16[1536,1408]{1,0:T(8,128)(2,1)} fusion(bf16[1536,1408]{1,0:T(8,128)(2,1)} %bitcast.147, s32[2048]{0:T(1024)S(1)} %pad_clamp_fusion), kind=kCustom, calls=%fused_computation.2 | custom fusion | bytes 8656896 | tf_op jit(solution)/shard_map/gather | solution.py:104
  159.7 3.1 fusion.56
  162.8 5.3 fusion.77
  168.1 51.9 %all-gather.14.cloned.1.call-done = bf16[1408,1408]{1,0:T(8,128)(2,1)} async-done(((bf16[176,1408]{1,0:T(8,128)(2,1)}), bf16[1408,1408]{1,0:T(8,128)(2,1)}) %all-gather.14.cloned.1.call-update) | async-done | bytes 3964944 | tf_op jit(solution)/shard_map/all_gather | solution.py:68
  219.9 5.4 convolution_convert_fusion.4
  226.6 6.6 %fusion.8 = (f32[4,4,384]{2,1,0:T(4,128)S(1)}, bf16[4,4,384,384]{2,3,1,0:T(8,128)(2,1)S(1)}, bf16[4,4,384,384]{2,3,1,0:T(8,128)(2,1)}) fusion(f32[4,4,384,384]{2,3,1,0:T(8,128)} %get-tuple-element.46, f32[4,4,384]{2,1,0:T(4,128)S(1)} %multiply_divide_fusion, f32[4,4,384]{2,1,0:T(4,128)S(1)} %get-tuple-element.45, bf16[4,384,4,88]{1,0,3,2:T(4,128)(2,1)S(1)} %reshape.231, ...), kind=kOutput, calls=%fused_computation.16 | convolution fusion | flops 431745024 | bytes 21110784 | tf_op jit(solution)/shard_map/transpose(jvp(ahqk,akhd->aqhd))/dot_general | solution.py:41
  233.3 9.4 %fusion.38 = bf16[4,384,4,88]{1,3,2,0:T(8,128)(2,1)} fusion(bf16[4,384,4,88]{1,0,3,2:T(4,128)(2,1)} %reshape.232, f32[4,4,384,384]{2,3,1,0:T(8,128)} %get-tuple-element.46, bf16[4,4,384,384]{2,3,1,0:T(8,128)(2,1)} %get-tuple-element.47, f32[4,4,384]{2,1,0:T(4,128)S(1)} %neg.12, f32[4,4,384]{2,1,0:T(4,128)S(1)} %get-tuple-element.45, ...), kind=kOutput, calls=%fused_computation.68 | convolution fusion | flops 429932544 | bytes 16957440 | tf_op jit(solution)/shard_map/transpose(jvp(aqhd,akhd->ahqk))/dot_general | solution.py:36
  242.7 9.2 %fusion.39 = bf16[4,384,4,88]{1,3,2,0:T(8,128)(2,1)} fusion(bf16[4,384,4,88]{1,0,3,2:T(4,128)(2,1)} %reshape.233, f32[4,4,384,384]{2,3,1,0:T(8,128)} %get-tuple-element.46, bf16[4,4,384,384]{2,3,1,0:T(8,128)(2,1)} %get-tuple-element.47, f32[4,4,384]{2,1,0:T(4,128)S(1)} %neg.12, f32[4,4,384]{2,1,0:T(4,128)S(1)} %get-tuple-element.45, ...), kind=kOutput, calls=%fused_computation.69 | convolution fusion | flops 429932544 | bytes 16957440 | tf_op jit(solution)/shard_map/transpose(jvp(aqhd,akhd->ahqk))/dot_general | solution.py:36
  259.1 3.0 convolution_convert_fusion.3
  262.2 10.5 %convolution_convert_fusion.1 = bf16[1408,1056]{1,0:T(8,128)(2,1)} fusion(bf16[1536,352]{0,1:T(8,128)(2,1)S(1)} %bitcast.155, bf16[1536,352]{0,1:T(8,128)(2,1)S(1)} %bitcast.152, bf16[1536,352]{0,1:T(8,128)(2,1)S(1)} %bitcast.158, f32[1408]{0:T(1024)S(1)} %copy-done.10, f32[1408]{0:T(1024)S(1)} %copy-done.8, f32[1536]{0:T(1024)S(1)} %add_rsqrt_fusion, ...), kind=kOutput, calls=%fused_computation.26 | convolution fusion | flops 4591792128 | bytes 10566656 | tf_op jit(solution)/shard_map/dot_general | solution.py:120
  272.7 9.8 %convolution_convert_fusion = bf16[1536,1408]{1,0:T(8,128)(2,1)} fusion(bf16[1408,1056]{1,0:T(8,128)(2,1)} %all-gather.12.cloned.1.call-done, bf16[1536,352]{0,1:T(8,128)(2,1)S(1)} %bitcast.156, bf16[1536,352]{0,1:T(8,128)(2,1)S(1)} %bitcast.153, bf16[1536,352]{0,1:T(8,128)(2,1)S(1)} %bitcast.159), kind=kOutput, calls=%fused_computation.25 | convolution fusion | flops 4579491840 | bytes 10543104 | tf_op jit(solution)/shard_map/dot_general | solution.py:134
  282.5 5.0 all-to-all-start.1
  290.9 47.3 %all-reduce.6.cloned.1.call-done = bf16[352,1408]{1,0:T(8,128)(2,1)} async-done(((bf16[352,1408]{1,0:T(8,128)(2,1)}), bf16[352,1408]{1,0:T(8,128)(2,1)}) %all-reduce.6.cloned.1.call-update) | async-done | bytes 991248 | tf_op jit(solution)/shard_map/psum | solution.py:114
  340.5 3.5 reduce_sum.235
  347.6 5.3 gather_fusion
  352.9 2.3 copy.77
  355.3 3.5 all-to-all-start
  358.9 6.8 %gather_fusion.1 = bf16[384,1408]{1,0:T(8,128)(2,1)} fusion(bf16[1536,1408]{1,0:T(8,128)(2,1)} %bitcast.148, s32[1024]{0:T(1024)S(1)} %pad_clamp_fusion.2), kind=kCustom, calls=%fused_computation.1 | custom fusion | bytes 2164224 | tf_op jit(solution)/shard_map/gather | solution.py:152
  365.7 7.9 %all-to-all-done = bf16[4,384,352]{1,2,0:T(8,128)(2,1)S(1)} async-done(((bf16[4,384,352]{1,2,0:T(8,128)(2,1)}), bf16[4,384,352]{1,2,0:T(8,128)(2,1)S(1)}, u32[]{:S(2)}, u32[]{:S(2)}) %all-to-all-start) | async-done | bytes 1081376 | tf_op jit(solution)/shard_map/all_to_all | solution.py:147
  373.7 5.5 %fusion.20 = bf16[1,384,1408]{2,1,0:T(8,128)(2,1)} fusion(bf16[1408,1408]{1,0:T(8,128)(2,1)} %all-gather.14.cloned.1.call-done, bf16[384,1408]{1,0:T(8,128)(2,1)} %gather_fusion.1, bf16[384,352]{0,1:T(8,128)(2,1)S(1)} %get-tuple-element.35, bf16[384,352]{0,1:T(8,128)(2,1)S(1)} %get-tuple-element.36, bf16[384,352]{0,1:T(8,128)(2,1)S(1)} %get-tuple-element.37, ...), kind=kOutput, calls=%fused_computation.45 | convolution fusion | flops 1529020416 | bytes 7214592 | tf_op jit(solution)/shard_map/dot_general | solution.py:154
  379.2 36.3 %reduce-scatter.2.cloned.1.call-done = bf16[176,1056]{1,0:T(8,128)(2,1)} async-done(((bf16[1408,1056]{1,0:T(8,128)(2,1)}), bf16[176,1056]{1,0:T(8,128)(2,1)}) %reduce-scatter.2.cloned.1.call-update) | async-done | bytes 371728 | tf_op jit(solution)/shard_map/reduce_scatter | solution.py:123
  415.5 34.9 %all-reduce.8.cloned.1.call-done = bf16[176,1408]{1,0:T(8,128)(2,1)} async-done(((bf16[176,1408]{1,0:T(8,128)(2,1)}), bf16[176,1408]{1,0:T(8,128)(2,1)}) %all-reduce.8.cloned.1.call-update) | async-done | bytes 495632 | tf_op jit(solution)/shard_map/psum | solution.py:118
  452.9 3.1 fusion.40
  455.9 51.6 %all-gather.22.cloned.1.call-done = f32[32,1,8448]{2,1,0:T(1,128)} async-done(((f32[1,1,8448]{2,1,0:T(1,128)}), f32[32,1,8448]{2,1,0:T(1,128)}) %all-gather.22.cloned.1.call-update) | async-done | bytes 1081360 | tf_op jit(solution)/shard_map/all_gather | solution.py:162
  510.6 17.4 %all-gather.20.cloned.1.call-done = bf16[704,1056]{1,0:T(8,128)(2,1)} async-done(((bf16[176,1056]{1,0:T(8,128)(2,1)}), bf16[704,1056]{1,0:T(8,128)(2,1)}) %all-gather.20.cloned.1.call-update) | async-done | bytes 1486864 | tf_op jit(solution)/shard_map/all_gather | solution.py:124
  530.1 3.3 concatenate.18
  (130 shorter events, 38.5 us)
Async XLA Ops:
  7.2 4.5 copy-start.13
  7.2 4.5 copy-start.12
  7.2 10.6 %copy-start.9 = (f32[4224]{0:T(1024)S(1)}, f32[4224]{0:T(1024)}, u32[]{:S(2)}) copy-start(f32[4224]{0:T(1024)} %param.16) | copy-start | bytes 50692
  7.2 40.4 %all-gather.16.cloned.1.call-start = ((), (), s32[]{:S(2)}) async-start(), calls=%async_computation.8 | async-start | bytes 5406720 | tf_op jit(solution)/shard_map/all_gather | solution.py:65
  7.9 104.0 %all-gather.12.cloned.1.call-start = ((), (), s32[]{:S(2)}) async-start(), calls=%async_computation.3 | async-start | bytes 3649536 | tf_op jit(solution)/shard_map/all_gather | solution.py:66
  10.3 137.1 %all-gather.18.cloned.1.call-start = ((), (), s32[]{:S(2)}) async-start(), calls=%async_computation.9 | async-start | bytes 5406720 | tf_op jit(solution)/shard_map/all_gather | solution.py:67
  11.1 208.9 %all-gather.14.cloned.1.call-start = ((), (), s32[]{:S(2)}) async-start(), calls=%async_computation.4 | async-start | bytes 4460544 | tf_op jit(solution)/shard_map/all_gather | solution.py:68
  11.6 326.7 %all-reduce.6.cloned.1.call-start = ((), (), s32[]{:S(2)}) async-start(), calls=%async_computation.6 | async-start | bytes 1982464 | tf_op jit(solution)/shard_map/psum | solution.py:114
  47.6 3.5 copy-start
  50.6 61.4 %copy-start.8 = (f32[1408]{0:T(1024)S(1)}, f32[1408]{0:T(1024)}, u32[]{:S(2)}) copy-start(f32[1408]{0:T(1024)} %param.13) | copy-start | bytes 16900
  50.6 61.4 %copy-start.10 = (f32[1408]{0:T(1024)S(1)}, f32[1408]{0:T(1024)}, u32[]{:S(2)}) copy-start(f32[1408]{0:T(1024)} %param.14) | copy-start | bytes 16900
  159.7 3.1 copy-start.7
  253.9 1.2 copy-start.6
  253.9 2.0 copy-start.5
  255.2 3.9 slice-start
  256.6 2.5 slice-start.1
  257.4 15.4 %copy-start.2 = (bf16[44,8,4,384]{3,1,2,0:T(8,128)(2,1)}, bf16[44,8,4,384]{3,1,2,0:T(8,128)(2,1)S(1)}, u32[]{:S(2)}) copy-start(bf16[44,8,4,384]{3,1,2,0:T(8,128)(2,1)S(1)} %copy.95) | copy-start | bytes 3244036
  258.1 1.0 copy-start.4
  262.1 153.4 %reduce-scatter.2.cloned.1.call-start = ((), (), s32[]{:S(2)}) async-start(), calls=%async_computation.5 | async-start | bytes 3649536 | tf_op jit(solution)/shard_map/reduce_scatter | solution.py:123
  282.5 5.5 %copy-start.1 = (bf16[1,384,1408]{2,1,0:T(8,128)(2,1)S(1)}, bf16[1,384,1408]{2,1,0:T(8,128)(2,1)}, u32[]{:S(2)}) copy-start(bf16[1,384,1408]{2,1,0:T(8,128)(2,1)} %param.10) | copy-start | bytes 3244036
  282.5 58.0 %all-to-all-start.1 = ((bf16[4,384,1408]{2,1,0:T(8,128)(2,1)}), bf16[4,384,1408]{2,1,0:T(8,128)(2,1)}, u32[]{:S(2)}, u32[]{:S(2)}) async-start(bf16[4,384,1408]{2,1,0:T(8,128)(2,1)} %bitcast.161), calls=%async_computation.1 | async-start | bytes 8650752 | tf_op jit(solution)/shard_map/all_to_all | solution.py:137
  287.5 162.8 %all-reduce.8.cloned.1.call-start = ((), (), s32[]{:S(2)}) async-start(), calls=%async_computation.7 | async-start | bytes 991232 | tf_op jit(solution)/shard_map/psum | solution.py:118
  287.9 2.2 copy-start.3
  340.2 167.4 %all-gather.22.cloned.1.call-start = ((), (), s32[]{:S(2)}) async-start(), calls=%async_computation.11 | async-start | bytes 1115136 | tf_op jit(solution)/shard_map/all_gather | solution.py:162
  355.3 18.3 %all-to-all-start = ((bf16[4,384,352]{1,2,0:T(8,128)(2,1)}), bf16[4,384,352]{1,2,0:T(8,128)(2,1)S(1)}, u32[]{:S(2)}, u32[]{:S(2)}) async-start(bf16[4,384,352]{1,2,0:T(8,128)(2,1)} %copy.77), calls=%async_computation | async-start | bytes 2162688 | tf_op jit(solution)/shard_map/all_to_all | solution.py:147
  358.8 169.3 %all-gather.20.cloned.1.call-start = ((), (), s32[]{:S(2)}) async-start(), calls=%async_computation.10 | async-start | bytes 2027520 | tf_op jit(solution)/shard_map/all_gather | solution.py:124
  358.9 14.8 %copy-start.11 = (f32[1408]{0:T(1024)S(1)}, f32[1408]{0:T(1024)}, u32[]{:S(2)}) copy-start(f32[1408]{0:T(1024)} %param.18) | copy-start | bytes 16900
Sparse Core Ops, SparseCore 0:
  9.6 37.9 all-gather.15
  50.3 61.5 all-gather.11
  113.5 33.8 all-gather.17
  149.4 70.4 all-gather.13
  262.2 76.0 all-reduce.5
  341.8 73.6 reduce-scatter.1
  418.4 31.9 all-reduce.7
  453.3 54.2 all-gather.21
  509.1 18.8 all-gather.19

commit v2 on v1

--- a/solution.py
+++ b/solution.py
@@ -42,6 +42,11 @@
     return context.reshape(loaders * row_count, width).astype(jnp.bfloat16)
 
 
+def to_group(rows, dp_size):
+    copies = jnp.broadcast_to(rows[None], (dp_size,) + rows.shape)
+    return lax.all_to_all(copies, "dp", 0, 0, tiled=True).reshape(-1, rows.shape[1])
+
+
 def per_device(tokens, patches, owners, ln_gain, ln_shift, w_qkv, b_qkv, w_proj, b_proj, grad_out):
     own_tokens = tokens[0]
     row_count, model_width = own_tokens.shape
@@ -62,10 +67,23 @@
     )
     b_part = lax.dynamic_slice_in_dim(b_qkv.reshape(3, dp_size, width), me, 1, axis=1).reshape(-1)
 
-    all_tokens = lax.all_gather(own_tokens, "dp", axis=0, tiled=True)
+    piece_rows = shard_rows // dp_size
+    per_block = width // shard_rows
+    to_heads = [
+        (d * fsdp_size + f, (f // per_block) * fsdp_size + (f % per_block) * dp_size + d)
+        for d in range(dp_size)
+        for f in range(fsdp_size)
+    ]
+    to_shards = [(there, here) for here, there in to_heads]
+    own_piece = lax.dynamic_index_in_dim(
+        w_proj.reshape(dp_size, piece_rows, model_width), me, 0, keepdims=False
+    )
+    head_piece = lax.ppermute(own_piece, ("dp", "fsdp"), to_heads)
+
+    all_tokens = to_group(own_tokens, dp_size)
     w_heads = lax.all_gather(w_part, "fsdp", axis=0, tiled=True)
-    all_grad = lax.all_gather(grad_out[0], "dp", axis=0, tiled=True)
-    w_full = lax.all_gather(w_proj, "fsdp", axis=0, tiled=True)
+    all_grad = to_group(grad_out[0], dp_size)
+    w_rows = lax.all_gather(head_piece, "fsdp", axis=0).reshape(width, model_width)
     tables = lax.all_gather(
         jnp.concatenate([patches, owners], axis=2), "dp", axis=1, tiled=True
     )[0]
@@ -102,7 +120,6 @@
     )
     context, attend_back = jax.vjp(partial(attend, same_image, head_count), joined)
     grad_rows = all_grad[destination]
-    w_rows = lax.dynamic_slice_in_dim(w_full, me * width, width, 0)
     grad_context = lax.dot_general(
         grad_rows, w_rows, (((1,), (1,)), ((), ())), preferred_element_type=jnp.float32
     ).astype(jnp.bfloat16)
@@ -111,17 +128,20 @@
     term_proj = lax.dot_general(
         context, grad_rows, (((0,), (0,)), ((), ())), preferred_element_type=jnp.float32
     ).astype(jnp.bfloat16)
-    rows_proj = lax.psum(term_proj, "fsdp")
-    per_block = width // shard_rows
-    mine = lax.dynamic_slice_in_dim(rows_proj, (shard % per_block) * shard_rows, shard_rows, 0)
-    mine = jnp.where(shard // per_block == me, mine, jnp.zeros((), mine.dtype))
-    summed_proj = lax.psum(mine, "dp")
+    pieces = lax.all_to_all(
+        term_proj.reshape(fsdp_size, piece_rows, model_width), "fsdp", 0, 0, tiled=True
+    )
+    piece_proj = jnp.sum(pieces.astype(jnp.float32), axis=0).astype(jnp.bfloat16)
+    piece_proj = lax.ppermute(piece_proj, ("dp", "fsdp"), to_shards)
 
     term_qkv = lax.dot_general(
         normed, grad_joined, (((0,), (0,)), ((), ())), preferred_element_type=jnp.float32
     ).astype(jnp.bfloat16)
     shard_qkv = lax.psum_scatter(term_qkv, "fsdp", scatter_dimension=0, tiled=True)
-    all_qkv = lax.all_gather(shard_qkv, "dp", axis=0)
+    sums = jnp.concatenate([shard_qkv, piece_proj.reshape(shard_rows, width)], axis=1)
+    all_sums = lax.all_gather(sums, "dp", axis=0)
+    all_qkv = all_sums[:, :, : 3 * width]
+    summed_proj = all_sums[:, :, 3 * width :].reshape(shard_rows, model_width)
     summed_qkv = jnp.concatenate(
         [
             all_qkv[peer, :, part * width : (part + 1) * width]
@@ -144,26 +164,32 @@
     _, norm_back = jax.vjp(layer_norm, own_tokens, ln_gain, ln_shift)
     grad_tokens, gain_term, shift_term = norm_back((grad_normed, own_grad))
 
-    context_out = lax.all_to_all(
-        context[origin.reshape(-1)].reshape(dp_size, row_count, width), "dp", 0, 0, tiled=True
-    )
-    own_context = jnp.concatenate([context_out[peer] for peer in range(dp_size)], axis=1)
+    part_out = jnp.dot(
+        context[origin.reshape(-1)], w_rows, preferred_element_type=jnp.float32
+    ).astype(jnp.bfloat16)
+    parts_out = lax.all_to_all(
+        part_out.reshape(dp_size, row_count, model_width), "dp", 0, 0, tiled=True
+    )
     own_origin = lax.dynamic_slice_in_dim(origin, me, 1, 0)[0]
     owned = all_tokens[own_origin].astype(jnp.float32)
-    y_owned = (
-        jnp.dot(own_context, w_full, preferred_element_type=jnp.float32) + b_proj + owned
-    ).astype(jnp.bfloat16)
+    y_owned = (jnp.sum(parts_out.astype(jnp.float32), axis=0) + b_proj + owned).astype(
+        jnp.bfloat16
+    )
 
     bias_part = jnp.sum(grad_joined.astype(jnp.float32), axis=0).reshape(3, 1, width)
     bias_term = jnp.where(
         peers[None, :, None] == me, bias_part, jnp.zeros((), jnp.float32)
     ).reshape(-1)
     proj_term = jnp.sum(grad_out[0].astype(jnp.float32), axis=0)
-    small = lax.all_gather(
-        jnp.concatenate([gain_term, shift_term, bias_term, proj_term]), ("dp", "fsdp")
+    terms = jnp.concatenate([gain_term, shift_term, bias_term, proj_term])
+    spread = lax.all_to_all(
+        terms.reshape(dp_size * fsdp_size, -1), ("dp", "fsdp"), 0, 0, tiled=True
     )
     device_share = 1.0 / (dp_size * fsdp_size)
-    small = jnp.sum(small, axis=0) * device_share
+    share = jnp.sum(spread, axis=0, keepdims=True) * device_share
+    small = lax.all_to_all(
+        jnp.broadcast_to(share, spread.shape), ("dp", "fsdp"), 0, 0, tiled=True
+    ).reshape(-1)
     cuts = (model_width, 2 * model_width, 5 * model_width)
     gain, shift, qkv_bias, proj_bias = jnp.split(small, cuts)
     return (

time: 546 us -> 446 us (0.82)
  waiting for transfers between devices: 359 us -> 123 us
  blocking collectives: 5.97 us -> 87.1 us
  starting transfers between devices: 9.12 us -> 41.1 us
  other arithmetic: 30.6 us -> 45.5 us
  local copies, waits for them, and re-layouts: 47.2 us -> 55.2 us
    all_gather x5 -> x1, waiting for transfers between devices: 171 us -> 0.01 us  [per_device(): all_sums = lax.all_gather(sums, 'dp', axis=0)]
    psum x2 -> x0, waiting for transfers between devices: 82.2 us -> none  [the longest x1 47.3 us: per_device(): rows_proj = lax.psum(term_proj, 'fsdp')]
    all_to_all x1 -> x6, waiting for transfers between devices: 7.87 us -> 87 us  [the longest x2 47.7 us: to_group(): lax.all_to_all(copies, 'dp', 0, 0, tiled=True).reshape(-1, rows.shape[1])]
    all_gather x1, waiting for transfers between devices: 59.6 us -> 0.01 us  [per_device(): w_heads = lax.all_gather(w_part, 'fsdp', axis=0, tiled=True)]
    all_gather x1, blocking collectives: 5.97 us -> 49.7 us  [per_device(): lax.all_gather(jnp.concatenate([patches, owners], axis=2), 'dp', axis=1,...]
    all_gather x0 -> x1, blocking collectives: none -> 37.4 us  [per_device(): lax.all_gather(head_piece, 'fsdp', axis=0).reshape(width, model_width)]
    reduce_scatter x1, waiting for transfers between devices: 36.3 us -> 0.02 us  [per_device(): lax.psum_scatter(term_qkv, 'fsdp', scatter_dimension=0, tiled=True)]
    all_to_all x1, waiting for transfers between devices: 0.01 us -> 35.9 us  [per_device(): lax.all_to_all(part_normed.reshape(dp_size, row_count, model_width), 'dp'...]
  transfers between devices with their start and end apart: 11 -> 12, of which waited for: 10 -> 6; matrix products, arithmetic and copies ran while one was open for 19% -> 23% of each run, Pallas kernels for 0% -> 0%
where the time goes in v2:
time: 446 us; the launch traced here: 440 us
  waiting for transfers between devices  123 us (28%)
  blocking collectives  87.1 us (20%)
  matrix products  73.8 us (17%)
  local copies, waits for them, and re-layouts  55.2 us (12%)
  other arithmetic  45.5 us (10%)
  starting transfers between devices  41.1 us (9%)
  between operations  14.5 us (3%)
    all_gather x1, blocking collectives, per_device(): lax.all_gather(jnp.concatenate([patches, owners], axis=2), 'dp', axis=1,...  49.7 us
    all_to_all x2, waiting for transfers between devices, to_group(): lax.all_to_all(copies, 'dp', 0, 0, tiled=True).reshape(-1, rows.shape[1])  47.7 us
    all_gather x1, blocking collectives, per_device(): lax.all_gather(head_piece, 'fsdp', axis=0).reshape(width, model_width)  37.4 us
    all_to_all x1, waiting for transfers between devices, per_device(): lax.all_to_all(part_normed.reshape(dp_size, row_count, model_width), 'dp'...  35.9 us
    all_to_all x1, waiting for transfers between devices, per_device(): lax.all_to_all(part_out.reshape(dp_size, row_count, model_width), 'dp', 0...  29.5 us
    dot_general x3, matrix products, attend(): scores = jnp.einsum('aqhd,akhd->ahqk', queries, keys) * head_size ** (-0.5)  21 us
    gather x1, local copies, waits for them, and re-layouts, per_device(): grad_rows = all_grad[destination]  12.8 us
    dot_general x3, matrix products, attend(): context = jnp.einsum('ahqk,akhd->aqhd', weights.astype(jnp.float32), values)  11.9 us
  transfers between devices with their start and end apart: 12, of which 6 were waited for; matrix products, arithmetic and copies ran while one was open for 23% of the time, Pallas kernels for 0%

profile of v2, /device:TPU:0, one launch (start us, length us, event | category | flops | bytes accessed | tf_op | source)
XLA Modules:
  0.0 440.1 jit_solution(1593021115931161664)
XLA Ops:
  7.2 3.5 broadcast_in_dim.50
  10.7 4.9 %all-to-all-start = ((bf16[4,384,1408]{2,1,0:T(8,128)(2,1)}), bf16[4,384,1408]{2,1,0:T(8,128)(2,1)}, u32[]{:S(2)}, u32[]{:S(2)}) async-start(bf16[4,384,1408]{2,1,0:T(8,128)(2,1)} %broadcast_in_dim.50), calls=%async_computation | async-start | bytes 8650752 | tf_op jit(solution)/shard_map/all_to_all | solution.py:47
  18.2 47.7 %all-to-all-done = bf16[4,384,1408]{2,1,0:T(8,128)(2,1)} async-done(((bf16[4,384,1408]{2,1,0:T(8,128)(2,1)}), bf16[4,384,1408]{2,1,0:T(8,128)(2,1)}, u32[]{:S(2)}, u32[]{:S(2)}) %all-to-all-start) | async-done | bytes 4325408 | tf_op jit(solution)/shard_map/all_to_all | solution.py:47
  68.2 5.0 %all-to-all-start.2 = ((bf16[4,384,1408]{2,1,0:T(8,128)(2,1)}), bf16[4,384,1408]{2,1,0:T(8,128)(2,1)}, u32[]{:S(2)}, u32[]{:S(2)}) async-start(bf16[4,384,1408]{2,1,0:T(8,128)(2,1)} %broadcast_in_dim.54), calls=%async_computation.2 | async-start | bytes 8650752 | tf_op jit(solution)/shard_map/all_to_all | solution.py:47
  74.0 49.7 %all_gather.19 = s32[1,4,8]{2,0,1:T(1,128)S(1)} all-gather(s32[1,1,8]{2,0,1:T(1,128)S(1)} %pad_add_fusion.1), channel_id=1, replica_groups=mesh['dp'=4,'fsdp'=8] {'dp'}, dimensions={1}, use_global_device_ids=true | all-gather | bytes 160 | tf_op jit(solution)/shard_map/all_gather | solution.py:87
  126.1 37.4 %all-gather.2 = bf16[8,44,1408]{2,1,0:T(8,128)(2,1)S(1)} all-gather(bf16[1,44,1408]{2,1,0:T(8,128)(2,1)S(1)} %bitcast.155), channel_id=2, replica_groups=mesh['dp'=4,'fsdp'=8] {'fsdp'}, dimensions={0}, use_global_device_ids=true | all-gather | bytes 1115136 | tf_op jit(solution)/shard_map/all_gather | solution.py:86
  163.7 3.2 convert_reduce_fusion
  166.9 3.5 fusion.8
  170.5 12.8 %gather_fusion.2 = bf16[1536,1408]{1,0:T(8,128)(2,1)} fusion(bf16[1536,1408]{1,0:T(8,128)(2,1)} %bitcast.16, s32[2048]{0:T(1024)S(1)} %pad_clamp_fusion), kind=kCustom, calls=%fused_computation.2 | custom fusion | bytes 8656896 | tf_op jit(solution)/shard_map/gather | solution.py:122
  183.3 4.1 convolution_convert_fusion.5
  188.6 4.7 %add_convert_fusion = bf16[1536,1408]{1,0:T(8,128)(2,1)} fusion(f32[1408]{0:T(1024)S(1)} %copy-done.17, f32[1408]{0:T(1024)S(1)} %copy-done.14, f32[1536]{0:T(1024)S(1)} %rsqrt.22, f32[1536]{0:T(1024)S(1)} %div.47, bf16[4,384,1408]{2,1,0:T(8,128)(2,1)} %all-to-all-done), kind=kLoop, calls=%fused_computation.21 | loop fusion | flops 12976128 | bytes 8674304 | tf_op jit(solution)/shard_map/convert_element_type | solution.py:19
  193.3 8.1 %fusion.9 = bf16[1536,1056]{0,1:T(8,128)(2,1)S(1)} fusion(bf16[1536,1408]{1,0:T(8,128)(2,1)} %add_convert_fusion, bf16[1408,1056]{1,0:T(8,128)(2,1)} %all-gather.6.cloned.1.call-done, f32[1056]{0:T(1024)S(1)} %add.194), kind=kOutput, calls=%fused_computation.22 | convolution fusion | flops 4570841088 | bytes 10547328 | tf_op jit(solution)/shard_map/dot_general | solution.py:118
  207.1 8.1 %fusion.58 = (f32[4,4,384]{2,1,0:T(4,128)S(1)}, f32[4,4,384,384]{2,3,1,0:T(8,128)}) fusion(f32[4,4,384,384]{2,3,1,0:T(8,128)S(1)} %fusion.41, pred[4,384,384]{1,2,0:T(8,128)(4,1)} %broadcast_compare_fusion), kind=kOutput, calls=%fused_computation.147 | output fusion | flops 14156159 | bytes 19488768 | tf_op jit(solution)/shard_map/jvp()/sub | solution.py:39
  215.2 8.8 %fusion.6 = (f32[4,4,384]{2,1,0:T(4,128)S(1)}, bf16[4,4,384,384]{2,3,1,0:T(8,128)(2,1)S(1)}, bf16[4,4,384,384]{2,3,1,0:T(8,128)(2,1)}) fusion(f32[4,4,384,384]{2,3,1,0:T(8,128)} %get-tuple-element.42, f32[4,4,384]{2,1,0:T(4,128)S(1)} %multiply_divide_fusion, f32[4,4,384]{2,1,0:T(4,128)S(1)} %get-tuple-element.41, bf16[4,384,4,88]{1,0,3,2:T(4,128)(2,1)} %reshape.335, ...), kind=kOutput, calls=%fused_computation.14 | convolution fusion | flops 431745024 | bytes 21110784 | tf_op jit(solution)/shard_map/transpose(jvp(ahqk,akhd->aqhd))/dot_general | solution.py:41
  224.1 8.9 %fusion.32 = bf16[4,384,4,88]{1,3,2,0:T(8,128)(2,1)} fusion(bf16[4,384,4,88]{1,0,3,2:T(4,128)(2,1)S(1)} %copy-done.7, f32[4,4,384,384]{2,3,1,0:T(8,128)} %get-tuple-element.42, bf16[4,4,384,384]{2,3,1,0:T(8,128)(2,1)} %get-tuple-element.43, f32[4,4,384]{2,1,0:T(4,128)S(1)} %neg.12, f32[4,4,384]{2,1,0:T(4,128)S(1)} %get-tuple-element.41, ...), kind=kOutput, calls=%fused_computation.66 | convolution fusion | flops 429932544 | bytes 16957440 | tf_op jit(solution)/shard_map/transpose(jvp(aqhd,akhd->ahqk))/dot_general | solution.py:36
  233.0 9.4 %fusion.31 = bf16[4,384,4,88]{1,3,2,0:T(8,128)(2,1)} fusion(bf16[4,384,4,88]{1,0,3,2:T(4,128)(2,1)} %reshape.336, f32[4,4,384,384]{2,3,1,0:T(8,128)} %get-tuple-element.42, bf16[4,4,384,384]{2,3,1,0:T(8,128)(2,1)} %get-tuple-element.43, f32[4,4,384]{2,1,0:T(4,128)S(1)} %neg.12, f32[4,4,384]{2,1,0:T(4,128)S(1)} %get-tuple-element.41, ...), kind=kOutput, calls=%fused_computation.65 | convolution fusion | flops 429932544 | bytes 16957440 | tf_op jit(solution)/shard_map/transpose(jvp(aqhd,akhd->ahqk))/dot_general | solution.py:36
  254.1 5.4 %all-to-all-start.4 = ((bf16[8,44,1408]{2,1,0:T(8,128)(2,1)}), bf16[8,44,1408]{2,1,0:T(8,128)(2,1)}, u32[]{:S(2)}, u32[]{:S(2)}) async-start(bf16[8,44,1408]{2,1,0:T(8,128)(2,1)} %reshape.347), calls=%async_computation.5 | async-start | bytes 2162688 | tf_op jit(solution)/shard_map/all_to_all | solution.py:131
  259.5 9.7 %convolution_convert_fusion.1 = bf16[1408,1056]{1,0:T(8,128)(2,1)} fusion(bf16[1536,1408]{1,0:T(8,128)(2,1)} %add_convert_fusion, bf16[1536,352]{0,1:T(8,128)(2,1)S(1)} %bitcast.138, bf16[1536,352]{0,1:T(8,128)(2,1)S(1)} %bitcast.135, bf16[1536,352]{0,1:T(8,128)(2,1)S(1)} %bitcast.141), kind=kOutput, calls=%fused_computation.24 | convolution fusion | flops 4578816000 | bytes 10543104 | tf_op jit(solution)/shard_map/dot_general | solution.py:137
  269.3 9.8 %convolution_convert_fusion = bf16[1536,1408]{1,0:T(8,128)(2,1)} fusion(bf16[1408,1056]{1,0:T(8,128)(2,1)} %all-gather.6.cloned.1.call-done, bf16[1536,352]{0,1:T(8,128)(2,1)S(1)} %bitcast.139, bf16[1536,352]{0,1:T(8,128)(2,1)S(1)} %bitcast.136, bf16[1536,352]{0,1:T(8,128)(2,1)S(1)} %bitcast.142), kind=kOutput, calls=%fused_computation.23 | convolution fusion | flops 4579491840 | bytes 10543104 | tf_op jit(solution)/shard_map/dot_general | solution.py:154
  279.1 3.2 all-to-all-done.4
  282.3 5.1 %all-to-all-start.3 = ((bf16[4,384,1408]{2,1,0:T(8,128)(2,1)}), bf16[4,384,1408]{2,1,0:T(8,128)(2,1)}, u32[]{:S(2)}, u32[]{:S(2)}) async-start(bf16[4,384,1408]{2,1,0:T(8,128)(2,1)} %bitcast.145), calls=%async_computation.3 | async-start | bytes 8650752 | tf_op jit(solution)/shard_map/all_to_all | solution.py:157
  289.7 5.3 %gather_fusion = bf16[1536,352]{1,0:T(8,128)(2,1)} fusion(bf16[1536,352]{1,0:T(8,128)(2,1)S(1)} %copy.95, s32[2048]{0:T(1024)S(1)} %pad_clamp_fusion.1), kind=kCustom, calls=%fused_computation | custom fusion | bytes 2168832 | tf_op jit(solution)/shard_map/gather | solution.py:168
  295.0 6.2 %convolution_convert_fusion.2 = bf16[1536,1408]{1,0:T(8,128)(2,1)} fusion(bf16[1536,352]{1,0:T(8,128)(2,1)} %gather_fusion, bf16[352,1408]{1,0:T(8,128)(2,1)} %copy-done.11), kind=kOutput, calls=%fused_computation.25 | convolution fusion | flops 1524695040 | bytes 6397952 | tf_op jit(solution)/shard_map/dot_general | solution.py:167
  301.2 35.9 %all-to-all-done.3 = bf16[4,384,1408]{2,1,0:T(8,128)(2,1)} async-done(((bf16[4,384,1408]{2,1,0:T(8,128)(2,1)}), bf16[4,384,1408]{2,1,0:T(8,128)(2,1)}, u32[]{:S(2)}, u32[]{:S(2)}) %all-to-all-start.3) | async-done | bytes 4325408 | tf_op jit(solution)/shard_map/all_to_all | solution.py:157
  337.1 5.0 %all-to-all-start.1 = ((bf16[4,384,1408]{2,1,0:T(8,128)(2,1)}), bf16[4,384,1408]{2,1,0:T(8,128)(2,1)}, u32[]{:S(2)}, u32[]{:S(2)}) async-start(bf16[4,384,1408]{2,1,0:T(8,128)(2,1)} %bitcast.144), calls=%async_computation.1 | async-start | bytes 8650752 | tf_op jit(solution)/shard_map/all_to_all | solution.py:170
  344.3 6.8 %gather_fusion.1 = bf16[384,1408]{1,0:T(8,128)(2,1)} fusion(bf16[1536,1408]{1,0:T(8,128)(2,1)} %bitcast.1, s32[1024]{0:T(1024)S(1)} %pad_clamp_fusion.2), kind=kCustom, calls=%fused_computation.1 | custom fusion | bytes 2164224 | tf_op jit(solution)/shard_map/gather | solution.py:174
  355.2 3.5 reduce_sum.260
  363.0 29.5 %all-to-all-done.1 = bf16[4,384,1408]{2,1,0:T(8,128)(2,1)} async-done(((bf16[4,384,1408]{2,1,0:T(8,128)(2,1)}), bf16[4,384,1408]{2,1,0:T(8,128)(2,1)}, u32[]{:S(2)}, u32[]{:S(2)}) %all-to-all-start.1) | async-done | bytes 4325408 | tf_op jit(solution)/shard_map/all_to_all | solution.py:170
  392.5 10.3 %all-to-all-start.5 = ((f32[32,1,264]{2,1,0:T(1,128)}), f32[32,1,264]{2,1,0:T(1,128)S(1)}, u32[]{:S(2)}, u32[]{:S(2)}) async-start(f32[32,1,264]{2,1,0:T(1,128)} %all_to_all.30), calls=%async_computation.6 | async-start | bytes 98304 | tf_op jit(solution)/shard_map/all_to_all | solution.py:185
  402.9 3.6 convert_reduce_fusion.1
  410.9 3.9 all-to-all-start.6
  417.8 4.1 all-to-all-done.6
  (154 shorter events, 58.2 us)
Async XLA Ops:
  10.7 55.2 %all-to-all-start = ((bf16[4,384,1408]{2,1,0:T(8,128)(2,1)}), bf16[4,384,1408]{2,1,0:T(8,128)(2,1)}, u32[]{:S(2)}, u32[]{:S(2)}) async-start(bf16[4,384,1408]{2,1,0:T(8,128)(2,1)} %broadcast_in_dim.50), calls=%async_computation | async-start | bytes 8650752 | tf_op jit(solution)/shard_map/all_to_all | solution.py:47
  15.6 2.5 copy-start.13
  15.6 50.3 %copy-start.3 = (bf16[1,384,1408]{2,1,0:T(8,128)(2,1)S(1)}, bf16[1,384,1408]{2,1,0:T(8,128)(2,1)}, u32[]{:S(2)}) copy-start(bf16[1,384,1408]{2,1,0:T(8,128)(2,1)} %param.19) | copy-start | bytes 3244036
  15.6 177.7 %all-gather.6.cloned.1.call-start = ((), (), s32[]{:S(2)}) async-start(), calls=%async_computation.8 | async-start | bytes 3649536 | tf_op jit(solution)/shard_map/all_gather | solution.py:84
  68.2 5.0 %copy-start.18 = (s32[1,1,4]{2,1,0:T(1,128)S(1)}, s32[1,1,4]{2,1,0:T(1,128)}, u32[]{:S(2)}) copy-start(s32[1,1,4]{2,1,0:T(1,128)} %param.12) | copy-start | bytes 52
  68.2 5.1 %copy-start.19 = (s32[1,1,4]{2,1,0:T(1,128)S(1)}, s32[1,1,4]{2,1,0:T(1,128)}, u32[]{:S(2)}) copy-start(s32[1,1,4]{2,1,0:T(1,128)} %param.11) | copy-start | bytes 52
  68.2 57.7 %copy-start.15 = (f32[4224]{0:T(1024)S(1)}, f32[4224]{0:T(1024)}, u32[]{:S(2)}) copy-start(f32[4224]{0:T(1024)} %param.16) | copy-start | bytes 50692
  68.2 102.3 %all-to-all-start.2 = ((bf16[4,384,1408]{2,1,0:T(8,128)(2,1)}), bf16[4,384,1408]{2,1,0:T(8,128)(2,1)}, u32[]{:S(2)}, u32[]{:S(2)}) async-start(bf16[4,384,1408]{2,1,0:T(8,128)(2,1)} %broadcast_in_dim.54), calls=%async_computation.2 | async-start | bytes 8650752 | tf_op jit(solution)/shard_map/all_to_all | solution.py:47
  73.3 52.7 %collective-permute-start = (bf16[44,1408]{1,0:T(8,128)(2,1)S(1)}, bf16[44,1408]{1,0:T(8,128)(2,1)S(1)}, u32[]{:S(2)}, u32[]{:S(2)}) collective-permute-start(bf16[44,1408]{1,0:T(8,128)(2,1)S(1)} %dynamic-slice_bitcast_fusion), channel_id=1, source_target_pairs={{0,0},{1,4},{2,8},{3,12},{4,16},{5,20},{6,24},{7,28},{8,1},{9,5},{... | collective-permute-start | bytes 371720 | tf_op jit(solution)/shard_map/ppermute | solution.py:81
  163.7 19.6 %copy-start.11 = (bf16[352,1408]{1,0:T(8,128)(2,1)}, bf16[352,1408]{1,0:T(8,128)(2,1)S(1)}, u32[]{:S(2)}) copy-start(bf16[352,1408]{1,0:T(8,128)(2,1)S(1)} %reshape.379) | copy-start | bytes 2973700
  183.3 5.3 %copy-start.14 = (f32[1408]{0:T(1024)S(1)}, f32[1408]{0:T(1024)}, u32[]{:S(2)}) copy-start(f32[1408]{0:T(1024)} %param.13) | copy-start | bytes 16900
  183.3 5.3 %copy-start.17 = (f32[1408]{0:T(1024)S(1)}, f32[1408]{0:T(1024)}, u32[]{:S(2)}) copy-start(f32[1408]{0:T(1024)} %param.14) | copy-start | bytes 16900
  203.1 1.4 copy-start.6
  207.1 8.1 %copy-start.4 = (bf16[4,384,4,88]{1,0,3,2:T(4,128)(2,1)S(1)}, bf16[4,384,4,88]{1,0,3,2:T(4,128)(2,1)}, u32[]{:S(2)}) copy-start(bf16[4,384,4,88]{1,0,3,2:T(4,128)(2,1)} %reshape.342) | copy-start | bytes 3244036
  215.2 8.9 %copy-start.7 = (bf16[4,384,4,88]{1,0,3,2:T(4,128)(2,1)S(1)}, bf16[4,384,4,88]{1,0,3,2:T(4,128)(2,1)}, u32[]{:S(2)}) copy-start(bf16[4,384,4,88]{1,0,3,2:T(4,128)(2,1)} %copy-done.6) | copy-start | bytes 3244036
  215.2 8.9 %copy-start.12 = (pred[4,384,384]{1,2,0:T(8,128)(4,1)S(1)}, pred[4,384,384]{1,2,0:T(8,128)(4,1)}, u32[]{:S(2)}) copy-start(pred[4,384,384]{1,2,0:T(8,128)(4,1)} %broadcast_compare_fusion) | copy-start | bytes 1769476
  242.4 2.0 copy-start.5
  244.4 2.0 copy-start.9
  245.7 3.2 slice-start
  247.1 1.7 slice-start.1
  248.6 20.6 %copy-start.1 = (bf16[44,8,4,384]{3,1,2,0:T(8,128)(2,1)}, bf16[44,8,4,384]{3,1,2,0:T(8,128)(2,1)S(1)}, u32[]{:S(2)}) copy-start(bf16[44,8,4,384]{3,1,2,0:T(8,128)(2,1)S(1)} %copy.115) | copy-start | bytes 3244036
  254.1 28.3 %all-to-all-start.4 = ((bf16[8,44,1408]{2,1,0:T(8,128)(2,1)}), bf16[8,44,1408]{2,1,0:T(8,128)(2,1)}, u32[]{:S(2)}, u32[]{:S(2)}) async-start(bf16[8,44,1408]{2,1,0:T(8,128)(2,1)} %reshape.347), calls=%async_computation.5 | async-start | bytes 2162688 | tf_op jit(solution)/shard_map/all_to_all | solution.py:131
  259.5 99.3 %reduce-scatter.2.cloned.1.call-start = ((), (), s32[]{:S(2)}) async-start(), calls=%async_computation.9 | async-start | bytes 3649536 | tf_op jit(solution)/shard_map/reduce_scatter | solution.py:140
  282.3 54.8 %all-to-all-start.3 = ((bf16[4,384,1408]{2,1,0:T(8,128)(2,1)}), bf16[4,384,1408]{2,1,0:T(8,128)(2,1)}, u32[]{:S(2)}, u32[]{:S(2)}) async-start(bf16[4,384,1408]{2,1,0:T(8,128)(2,1)} %bitcast.145), calls=%async_computation.3 | async-start | bytes 8650752 | tf_op jit(solution)/shard_map/all_to_all | solution.py:157
  337.1 5.1 %copy-start = (bf16[1,384,1408]{2,1,0:T(8,128)(2,1)S(1)}, bf16[1,384,1408]{2,1,0:T(8,128)(2,1)}, u32[]{:S(2)}) copy-start(bf16[1,384,1408]{2,1,0:T(8,128)(2,1)} %param.10) | copy-start | bytes 3244036
  337.1 55.4 %all-to-all-start.1 = ((bf16[4,384,1408]{2,1,0:T(8,128)(2,1)}), bf16[4,384,1408]{2,1,0:T(8,128)(2,1)}, u32[]{:S(2)}, u32[]{:S(2)}) async-start(bf16[4,384,1408]{2,1,0:T(8,128)(2,1)} %bitcast.144), calls=%async_computation.1 | async-start | bytes 8650752 | tf_op jit(solution)/shard_map/all_to_all | solution.py:170
  342.1 81.3 %all-gather.8.cloned.1.call-start = ((), (), s32[]{:S(2)}) async-start(), calls=%async_computation.10 | async-start | bytes 2478080 | tf_op jit(solution)/shard_map/all_gather | solution.py:142
  354.2 0.8 collective-permute-start.1
  392.5 17.7 %all-to-all-start.5 = ((f32[32,1,264]{2,1,0:T(1,128)}), f32[32,1,264]{2,1,0:T(1,128)S(1)}, u32[]{:S(2)}, u32[]{:S(2)}) async-start(f32[32,1,264]{2,1,0:T(1,128)} %all_to_all.30), calls=%async_computation.6 | async-start | bytes 98304 | tf_op jit(solution)/shard_map/all_to_all | solution.py:185
  402.8 3.6 copy-start.8
  402.8 3.6 copy-start.16
  410.9 11.1 %all-to-all-start.6 = ((f32[32,1,264]{2,1,0:T(1,128)}), f32[32,1,264]{2,1,0:T(1,128)S(1)}, u32[]{:S(2)}, u32[]{:S(2)}) async-start(f32[32,1,264]{2,1,0:T(1,128)} %broadcast_in_dim.71), calls=%async_computation.7 | async-start | bytes 98304 | tf_op jit(solution)/shard_map/all_to_all | solution.py:190
  (2 other events, 2.2 us)
Sparse Core Ops, SparseCore 0:
  19.2 72.2 all-gather.5
  269.4 74.8 reduce-scatter.1
  360.8 57.7 all-gather.7

commit v3 on v2

--- a/solution.py
+++ b/solution.py
@@ -80,13 +80,21 @@
     )
     head_piece = lax.ppermute(own_piece, ("dp", "fsdp"), to_heads)
 
-    all_tokens = to_group(own_tokens, dp_size)
-    w_heads = lax.all_gather(w_part, "fsdp", axis=0, tiled=True)
-    all_grad = to_group(grad_out[0], dp_size)
-    w_rows = lax.all_gather(head_piece, "fsdp", axis=0).reshape(width, model_width)
     tables = lax.all_gather(
         jnp.concatenate([patches, owners], axis=2), "dp", axis=1, tiled=True
     )[0]
+    own_tokens, tables = lax.optimization_barrier((own_tokens, tables))
+    all_tokens = to_group(own_tokens, dp_size)
+    weights = lax.all_gather(
+        jnp.concatenate([w_part, head_piece.reshape(shard_rows, width)], axis=1),
+        "fsdp",
+        axis=0,
+        tiled=True,
+    )
+    w_heads = weights[:, : 3 * width]
+    w_rows = weights[:, 3 * width :].reshape(width, model_width)
+    late_grad, all_tokens = lax.optimization_barrier((grad_out[0], all_tokens))
+    all_grad = to_group(late_grad, dp_size)
     lengths, targets = tables[:, :dp_size], tables[:, dp_size:]
 
     positions = jnp.arange(row_count, dtype=jnp.int32)
@@ -119,10 +127,18 @@
         jnp.bfloat16
     )
     context, attend_back = jax.vjp(partial(attend, same_image, head_count), joined)
+    context, all_grad = lax.optimization_barrier((context, all_grad))
     grad_rows = all_grad[destination]
     grad_context = lax.dot_general(
         grad_rows, w_rows, (((1,), (1,)), ((), ())), preferred_element_type=jnp.float32
     ).astype(jnp.bfloat16)
+    part_out = jnp.dot(
+        context[origin.reshape(-1)], w_rows, preferred_element_type=jnp.float32
+    ).astype(jnp.bfloat16)
+    grad_context, part_out = lax.optimization_barrier((grad_context, part_out))
+    parts_out = lax.all_to_all(
+        part_out.reshape(dp_size, row_count, model_width), "dp", 0, 0, tiled=True
+    )
     (grad_joined,) = attend_back(grad_context)
 
     term_proj = lax.dot_general(
@@ -154,6 +170,7 @@
     part_normed = lax.dot_general(
         grad_joined, w_heads, (((1,), (1,)), ((), ())), preferred_element_type=jnp.float32
     ).astype(jnp.bfloat16)
+    part_normed, parts_out = lax.optimization_barrier((part_normed, parts_out))
     parts = lax.all_to_all(
         part_normed.reshape(dp_size, row_count, model_width), "dp", 0, 0, tiled=True
     )
@@ -164,12 +181,6 @@
     _, norm_back = jax.vjp(layer_norm, own_tokens, ln_gain, ln_shift)
     grad_tokens, gain_term, shift_term = norm_back((grad_normed, own_grad))
 
-    part_out = jnp.dot(
-        context[origin.reshape(-1)], w_rows, preferred_element_type=jnp.float32
-    ).astype(jnp.bfloat16)
-    parts_out = lax.all_to_all(
-        part_out.reshape(dp_size, row_count, model_width), "dp", 0, 0, tiled=True
-    )
     own_origin = lax.dynamic_slice_in_dim(origin, me, 1, 0)[0]
     owned = all_tokens[own_origin].astype(jnp.float32)
     y_owned = (jnp.sum(parts_out.astype(jnp.float32), axis=0) + b_proj + owned).astype(

time: 446 us -> 397 us (0.89)
  blocking collectives: 87.1 us -> 16.8 us
  local copies, waits for them, and re-layouts: 55.2 us -> 67.5 us
  waiting for transfers between devices: 123 us -> 134 us
    all_gather x1 -> x0, blocking collectives: 37.4 us -> none  [per_device(): lax.all_gather(head_piece, 'fsdp', axis=0).reshape(width, model_width)]
    all_gather x1, blocking collectives: 49.7 us -> 16.8 us  [per_device(): lax.all_gather(jnp.concatenate([patches, owners], axis=2), 'dp', axis=1,...]
    all_to_all x1, waiting for transfers between devices: 3.21 us -> 16.5 us  [per_device(): lax.all_to_all(term_proj.reshape(fsdp_size, piece_rows, model_width), 'fs...]
    all_to_all x1, waiting for transfers between devices: 35.9 us -> 30.8 us  [per_device(): lax.all_to_all(part_normed.reshape(dp_size, row_count, model_width), 'dp'...]
    unnamed x51 -> x48, local copies, waits for them, and re-layouts: 1.37 us -> 6.05 us
  transfers between devices with their start and end apart: 12 -> 12, of which waited for: 6 -> 6; matrix products, arithmetic and copies ran while one was open for 23% -> 29% of each run, Pallas kernels for 0% -> 0%
where the time goes in v3:
time: 397 us; the launch traced here: 393 us
  waiting for transfers between devices  134 us (34%)
  matrix products  76 us (19%)
  local copies, waits for them, and re-layouts  67.5 us (17%)
  other arithmetic  43.8 us (11%)
  starting transfers between devices  40.2 us (10%)
  blocking collectives  16.8 us (4%)
  between operations  14.9 us (4%)
    all_to_all x2, waiting for transfers between devices, to_group(): lax.all_to_all(copies, 'dp', 0, 0, tiled=True).reshape(-1, rows.shape[1])  46.9 us
    all_to_all x1, waiting for transfers between devices, per_device(): lax.all_to_all(part_normed.reshape(dp_size, row_count, model_width), 'dp'...  30.8 us
    all_to_all x1, waiting for transfers between devices, per_device(): lax.all_to_all(part_out.reshape(dp_size, row_count, model_width), 'dp', 0...  28.3 us
    dot_general x3, matrix products, attend(): scores = jnp.einsum('aqhd,akhd->ahqk', queries, keys) * head_size ** (-0.5)  22.4 us
    all_gather x1, blocking collectives, per_device(): lax.all_gather(jnp.concatenate([patches, owners], axis=2), 'dp', axis=1,...  16.8 us
    all_to_all x1, waiting for transfers between devices, per_device(): lax.all_to_all(term_proj.reshape(fsdp_size, piece_rows, model_width), 'fs...  16.5 us
    gather x1, local copies, waits for them, and re-layouts, per_device(): grad_rows = all_grad[destination]  12.3 us
    sub x1, other arithmetic, attend(): exp_scores = jnp.exp(scores - row_peak)  10.9 us
  transfers between devices with their start and end apart: 12, of which 6 were waited for; matrix products, arithmetic and copies ran while one was open for 29% of the time, Pallas kernels for 0%

profile of v3, /device:TPU:0, one launch (start us, length us, event | category | flops | bytes accessed | tf_op | source)
XLA Modules:
  0.0 392.6 jit_solution(6829190984461327674)
XLA Ops:
  11.9 16.8 %all_gather.12 = s32[1,4,8]{2,0,1:T(1,128)S(1)} all-gather(s32[1,1,8]{2,0,1:T(1,128)S(1)} %pad_add_fusion.1), channel_id=1, replica_groups=mesh['dp'=4,'fsdp'=8] {'dp'}, dimensions={1}, use_global_device_ids=true | all-gather | bytes 160 | tf_op jit(solution)/shard_map/all_gather | solution.py:83
  31.0 5.1 %all-to-all-start = ((bf16[4,384,1408]{2,1,0:T(8,128)(2,1)}), bf16[4,384,1408]{2,1,0:T(8,128)(2,1)}, u32[]{:S(2)}, u32[]{:S(2)}) async-start(bf16[4,384,1408]{2,1,0:T(8,128)(2,1)} %broadcast_in_dim.44), calls=%async_computation | async-start | bytes 8650752 | tf_op jit(solution)/shard_map/all_to_all | solution.py:47
  39.0 46.9 %all-to-all-done = bf16[4,384,1408]{2,1,0:T(8,128)(2,1)} async-done(((bf16[4,384,1408]{2,1,0:T(8,128)(2,1)}), bf16[4,384,1408]{2,1,0:T(8,128)(2,1)}, u32[]{:S(2)}, u32[]{:S(2)}) %all-to-all-start) | async-done | bytes 4325408 | tf_op jit(solution)/shard_map/all_to_all | solution.py:47
  88.2 5.1 %all-to-all-start.1 = ((bf16[4,384,1408]{2,1,0:T(8,128)(2,1)}), bf16[4,384,1408]{2,1,0:T(8,128)(2,1)}, u32[]{:S(2)}, u32[]{:S(2)}) async-start(bf16[4,384,1408]{2,1,0:T(8,128)(2,1)} %broadcast_in_dim.47), calls=%async_computation.1 | async-start | bytes 8650752 | tf_op jit(solution)/shard_map/all_to_all | solution.py:47
  96.2 3.5 fusion.9
  99.8 9.0 %fusion.13 = bf16[1536,1056]{0,1:T(8,128)(2,1)S(1)} fusion(f32[1056]{0:T(1024)S(1)} %add.193, bf16[1408,1408]{1,0:T(8,128)(2,1)} %all-gather.4.cloned.1.call-done, bf16[1536,1408]{1,0:T(8,128)(2,1)} %bitcast.5, f32[1408]{0:T(1024)S(1)} %copy-done.18, f32[1408]{0:T(1024)S(1)} %copy-done.15, f32[1536]{0:T(1024)S(1)} %add_rsqrt_fusion, ...), kind=kOutput, calls=%fused_computation.25 | convolution fusion | flops 4583817216 | bytes 10841216 | tf_op jit(solution)/shard_map/dot_general | solution.py:126
  112.7 3.5 reshape.326
  121.1 6.3 %fusion.47 = f32[4,4,384,384]{2,3,1,0:T(8,128)} fusion(bf16[4,384,4,88]{1,0,3,2:T(4,128)(2,1)S(1)} %copy-done.8, bf16[4,384,4,88]{1,0,3,2:T(4,128)(2,1)} %reshape.323), kind=kOutput, calls=%fused_computation.82 | convolution fusion | flops 415236096 | bytes 11599872 | tf_op jit(solution)/shard_map/jvp(aqhd,akhd->ahqk)/dot_general | solution.py:36
  127.4 10.9 %fusion.67 = (f32[4,4,384]{2,1,0:T(4,128)S(1)}, f32[4,4,384,384]{2,3,1,0:T(8,128)S(1)}) fusion(f32[4,4,384,384]{2,3,1,0:T(8,128)} %fusion.47, pred[4,384,384]{1,2,0:T(8,128)(4,1)} %broadcast_compare_fusion), kind=kOutput, calls=%fused_computation.153 | output fusion | flops 14156159 | bytes 19488768 | tf_op jit(solution)/shard_map/jvp()/sub | solution.py:39
  145.6 12.3 %gather_fusion = bf16[1536,1408]{1,0:T(8,128)(2,1)} fusion(bf16[1536,1408]{1,0:T(8,128)(2,1)} %bitcast.8, s32[2048]{0:T(1024)S(1)} %pad_clamp_fusion.1), kind=kCustom, calls=%fused_computation | custom fusion | bytes 8656896 | tf_op jit(solution)/shard_map/gather | solution.py:131
  158.0 5.4 %gather_fusion.1 = bf16[1536,352]{1,0:T(8,128)(2,1)} fusion(bf16[1536,352]{1,0:T(8,128)(2,1)S(1)} %copy.95, s32[2048]{0:T(1024)S(1)} %pad_clamp_fusion), kind=kCustom, calls=%fused_computation.1 | custom fusion | bytes 2168832 | tf_op jit(solution)/shard_map/gather | solution.py:136
  163.4 4.5 %convolution_convert_fusion.5 = bf16[1536,352]{0,1:T(8,128)(2,1)S(1)} fusion(bf16[1536,1408]{1,0:T(8,128)(2,1)} %gather_fusion, bf16[352,1408]{1,0:T(8,128)(2,1)} %reshape.326), kind=kOutput, calls=%fused_computation.43 | convolution fusion | flops 1523073024 | bytes 6397952 | tf_op jit(solution)/shard_map/dot_general | solution.py:132
  168.0 4.1 %convolution_convert_fusion.2 = bf16[1536,1408]{1,0:T(8,128)(2,1)} fusion(bf16[1536,352]{1,0:T(8,128)(2,1)S(1)} %copy-done.11, bf16[352,1408]{1,0:T(8,128)(2,1)S(1)} %copy-done.14), kind=kOutput, calls=%fused_computation.28 | convolution fusion | flops 1524695040 | bytes 6397952 | tf_op jit(solution)/shard_map/dot_general | solution.py:135
  172.4 4.4 %fusion.36 = bf16[4,384,4,88]{1,3,2,0:T(8,128)(2,1)S(1)} fusion(bf16[4,4,384,384]{2,3,1,0:T(8,128)(2,1)} %copy-done, bf16[4,384,4,88]{1,0,3,2:T(4,128)(2,1)S(1)} %reshape.327), kind=kOutput, calls=%fused_computation.69 | convolution fusion | flops 415776768 | bytes 6881280 | tf_op jit(solution)/shard_map/transpose(jvp(ahqk,akhd->aqhd))/dot_general | solution.py:41
  176.7 4.7 %fusion.8 = (f32[4,4,384]{2,1,0:T(4,128)S(1)}, bf16[4,4,384,384]{2,3,1,0:T(8,128)(2,1)S(1)}) fusion(f32[4,4,384,384]{2,3,1,0:T(8,128)} %copy-done.2, f32[4,4,384]{2,1,0:T(4,128)S(1)} %multiply_divide_fusion, bf16[4,384,4,88]{1,0,3,2:T(4,128)(2,1)S(1)} %copy-done.4, bf16[4,384,4,88]{1,0,3,2:T(4,128)(2,1)S(1)} %reshape.327), kind=kOutput, calls=%fused_computation.16 | convolution fusion | flops 427026432 | bytes 16367616 | tf_op jit(solution)/shard_map/transpose(jvp(ahqk,akhd->aqhd))/dot_general | solution.py:41
  181.5 8.2 %fusion.38 = bf16[4,384,4,88]{1,3,2,0:T(8,128)(2,1)} fusion(bf16[4,384,4,88]{1,0,3,2:T(4,128)(2,1)} %reshape.324, f32[4,4,384,384]{2,3,1,0:T(8,128)} %copy-done.2, bf16[4,4,384,384]{2,3,1,0:T(8,128)(2,1)S(1)} %get-tuple-element.62, f32[4,4,384]{2,1,0:T(4,128)S(1)} %neg.12, f32[4,4,384]{2,1,0:T(4,128)S(1)} %get-tuple-element.59, ...), kind=kOutput, calls=%fused_computation.71 | convolution fusion | flops 429932544 | bytes 16957440 | tf_op jit(solution)/shard_map/transpose(jvp(aqhd,akhd->ahqk))/dot_general | solution.py:36
  189.7 7.9 %fusion.37 = bf16[4,384,4,88]{1,3,2,0:T(8,128)(2,1)} fusion(bf16[4,384,4,88]{1,0,3,2:T(4,128)(2,1)S(1)} %copy-done.9, f32[4,4,384,384]{2,3,1,0:T(8,128)} %copy-done.2, bf16[4,4,384,384]{2,3,1,0:T(8,128)(2,1)S(1)} %get-tuple-element.62, f32[4,4,384]{2,1,0:T(4,128)S(1)} %neg.12, f32[4,4,384]{2,1,0:T(4,128)S(1)} %get-tuple-element.59, ...), kind=kOutput, calls=%fused_computation.70 | convolution fusion | flops 429932544 | bytes 16957440 | tf_op jit(solution)/shard_map/transpose(jvp(aqhd,akhd->ahqk))/dot_general | solution.py:36
  198.4 5.0 %all-to-all-start.2 = ((bf16[4,384,1408]{2,1,0:T(8,128)(2,1)}), bf16[4,384,1408]{2,1,0:T(8,128)(2,1)}, u32[]{:S(2)}, u32[]{:S(2)}) async-start(bf16[4,384,1408]{2,1,0:T(8,128)(2,1)} %bitcast.136), calls=%async_computation.2 | async-start | bytes 8650752 | tf_op jit(solution)/shard_map/all_to_all | solution.py:139
  206.6 10.5 %convolution_convert_fusion.1 = bf16[1408,1056]{1,0:T(8,128)(2,1)} fusion(bf16[1536,352]{0,1:T(8,128)(2,1)S(1)} %bitcast.132, bf16[1536,352]{0,1:T(8,128)(2,1)S(1)} %bitcast.129, bf16[1536,352]{0,1:T(8,128)(2,1)S(1)} %bitcast.126, bf16[1536,1408]{1,0:T(8,128)(2,1)} %bitcast.5, f32[1408]{0:T(1024)S(1)} %copy-done.18, f32[1408]{0:T(1024)S(1)} %copy-done.15, ...), kind=kOutput, calls=%fused_computation.27 | convolution fusion | flops 4591792128 | bytes 10566656 | tf_op jit(solution)/shard_map/dot_general | solution.py:153
  217.2 5.3 %convolution_convert_fusion.4 = bf16[352,1408]{1,0:T(8,128)(2,1)} fusion(bf16[1536,352]{0,1:T(8,128)(2,1)} %bitcast.138, bf16[1536,1408]{1,0:T(8,128)(2,1)} %gather_fusion), kind=kOutput, calls=%fused_computation.42 | convolution fusion | flops 1523027968 | bytes 6397952 | tf_op jit(solution)/shard_map/dot_general | solution.py:144
  224.8 28.3 %all-to-all-done.2 = bf16[4,384,1408]{2,1,0:T(8,128)(2,1)} async-done(((bf16[4,384,1408]{2,1,0:T(8,128)(2,1)}), bf16[4,384,1408]{2,1,0:T(8,128)(2,1)}, u32[]{:S(2)}, u32[]{:S(2)}) %all-to-all-start.2) | async-done | bytes 4325408 | tf_op jit(solution)/shard_map/all_to_all | solution.py:139
  253.1 6.5 %all-to-all-start.4 = ((bf16[8,44,1408]{2,1,0:T(8,128)(2,1)}), bf16[8,44,1408]{2,1,0:T(8,128)(2,1)}, u32[]{:S(2)}, u32[]{:S(2)}) async-start(bf16[8,44,1408]{2,1,0:T(8,128)(2,1)} %reshape.333), calls=%async_computation.5 | async-start | bytes 2162688 | tf_op jit(solution)/shard_map/all_to_all | solution.py:147
  259.6 10.0 %convolution_convert_fusion = bf16[1536,1408]{1,0:T(8,128)(2,1)} fusion(bf16[1408,1408]{1,0:T(8,128)(2,1)} %all-gather.4.cloned.1.call-done, bf16[1536,352]{0,1:T(8,128)(2,1)} %bitcast.133, bf16[1536,352]{0,1:T(8,128)(2,1)S(1)} %bitcast.130, bf16[1536,352]{0,1:T(8,128)(2,1)S(1)} %bitcast.127), kind=kOutput, calls=%fused_computation.26 | convolution fusion | flops 4579491840 | bytes 10813440 | tf_op jit(solution)/shard_map/dot_general | solution.py:170
  269.5 16.5 %all-to-all-done.4 = bf16[8,44,1408]{2,1,0:T(8,128)(2,1)} async-done(((bf16[8,44,1408]{2,1,0:T(8,128)(2,1)}), bf16[8,44,1408]{2,1,0:T(8,128)(2,1)}, u32[]{:S(2)}, u32[]{:S(2)}) %all-to-all-start.4) | async-done | bytes 991264 | tf_op jit(solution)/shard_map/all_to_all | solution.py:147
  286.0 5.2 %all-to-all-start.3 = ((bf16[4,384,1408]{2,1,0:T(8,128)(2,1)}), bf16[4,384,1408]{2,1,0:T(8,128)(2,1)}, u32[]{:S(2)}, u32[]{:S(2)}) async-start(bf16[4,384,1408]{2,1,0:T(8,128)(2,1)} %bitcast.135), calls=%async_computation.3 | async-start | bytes 8650752 | tf_op jit(solution)/shard_map/all_to_all | solution.py:174
  293.4 6.8 %gather_fusion.2 = bf16[384,1408]{1,0:T(8,128)(2,1)} fusion(bf16[1536,1408]{1,0:T(8,128)(2,1)} %bitcast.5, s32[1024]{0:T(1024)S(1)} %pad_clamp_fusion.2), kind=kCustom, calls=%fused_computation.2 | custom fusion | bytes 2164224 | tf_op jit(solution)/shard_map/gather | solution.py:185
  306.4 3.2 convert_reduce_fusion.1
  310.8 30.8 %all-to-all-done.3 = bf16[4,384,1408]{2,1,0:T(8,128)(2,1)} async-done(((bf16[4,384,1408]{2,1,0:T(8,128)(2,1)}), bf16[4,384,1408]{2,1,0:T(8,128)(2,1)}, u32[]{:S(2)}, u32[]{:S(2)}) %all-to-all-start.3) | async-done | bytes 4325408 | tf_op jit(solution)/shard_map/all_to_all | solution.py:174
  341.6 3.5 reduce_sum.260
  346.9 9.1 %all-to-all-start.5 = ((f32[32,1,264]{2,1,0:T(1,128)}), f32[32,1,264]{2,1,0:T(1,128)S(1)}, u32[]{:S(2)}, u32[]{:S(2)}) async-start(f32[32,1,264]{2,1,0:T(1,128)} %all_to_all.30), calls=%async_computation.6 | async-start | bytes 98304 | tf_op jit(solution)/shard_map/all_to_all | solution.py:196
  356.5 6.8 %all-to-all-done.5 = f32[32,1,264]{2,1,0:T(1,128)S(1)} async-done(((f32[32,1,264]{2,1,0:T(1,128)}), f32[32,1,264]{2,1,0:T(1,128)S(1)}, u32[]{:S(2)}, u32[]{:S(2)}) %all-to-all-start.5) | async-done | bytes 33824 | tf_op jit(solution)/shard_map/all_to_all | solution.py:196
  369.6 4.2 %all-to-all-done.6 = f32[32,1,264]{2,1,0:T(1,128)S(1)} async-done(((f32[32,1,264]{2,1,0:T(1,128)}), f32[32,1,264]{2,1,0:T(1,128)S(1)}, u32[]{:S(2)}, u32[]{:S(2)}) %all-to-all-start.6) | async-done | bytes 33824 | tf_op jit(solution)/shard_map/all_to_all | solution.py:201
  (150 shorter events, 67.6 us)
Async XLA Ops:
  7.2 4.7 %copy-start.19 = (s32[1,1,4]{2,1,0:T(1,128)S(1)}, s32[1,1,4]{2,1,0:T(1,128)}, u32[]{:S(2)}) copy-start(s32[1,1,4]{2,1,0:T(1,128)} %param.12) | copy-start | bytes 52
  7.2 4.7 %copy-start.20 = (s32[1,1,4]{2,1,0:T(1,128)S(1)}, s32[1,1,4]{2,1,0:T(1,128)}, u32[]{:S(2)}) copy-start(s32[1,1,4]{2,1,0:T(1,128)} %param.11) | copy-start | bytes 52
  7.2 21.5 %copy-start.1 = (bf16[1,384,1408]{2,1,0:T(8,128)(2,1)S(1)}, bf16[1,384,1408]{2,1,0:T(8,128)(2,1)}, u32[]{:S(2)}) copy-start(bf16[1,384,1408]{2,1,0:T(8,128)(2,1)} %param.10) | copy-start | bytes 3244036
  7.2 92.5 %all-gather.4.cloned.1.call-start = ((), (), s32[]{:S(2)}) async-start(), calls=%async_computation.8 | async-start | bytes 4460544 | tf_op jit(solution)/shard_map/all_gather | solution.py:88
  8.5 2.0 collective-permute-start
  31.0 6.5 %copy-start.16 = (f32[4224]{0:T(1024)S(1)}, f32[4224]{0:T(1024)}, u32[]{:S(2)}) copy-start(f32[4224]{0:T(1024)} %param.16) | copy-start | bytes 50692
  31.0 54.9 %copy-start.7 = (bf16[1,384,1408]{2,1,0:T(8,128)(2,1)S(1)}, bf16[1,384,1408]{2,1,0:T(8,128)(2,1)}, u32[]{:S(2)}) copy-start(bf16[1,384,1408]{2,1,0:T(8,128)(2,1)} %param.19) | copy-start | bytes 3244036
  31.0 54.9 %all-to-all-start = ((bf16[4,384,1408]{2,1,0:T(8,128)(2,1)}), bf16[4,384,1408]{2,1,0:T(8,128)(2,1)}, u32[]{:S(2)}, u32[]{:S(2)}) async-start(bf16[4,384,1408]{2,1,0:T(8,128)(2,1)} %broadcast_in_dim.44), calls=%async_computation | async-start | bytes 8650752 | tf_op jit(solution)/shard_map/all_to_all | solution.py:47
  88.2 56.7 %all-to-all-start.1 = ((bf16[4,384,1408]{2,1,0:T(8,128)(2,1)}), bf16[4,384,1408]{2,1,0:T(8,128)(2,1)}, u32[]{:S(2)}, u32[]{:S(2)}) async-start(bf16[4,384,1408]{2,1,0:T(8,128)(2,1)} %broadcast_in_dim.47), calls=%async_computation.1 | async-start | bytes 8650752 | tf_op jit(solution)/shard_map/all_to_all | solution.py:47
  96.2 3.6 copy-start.15
  96.2 3.6 copy-start.18
  119.5 1.6 copy-start.8
  138.3 3.6 copy-start.2
  138.3 3.6 copy-start.3
  141.9 2.2 copy-start
  144.9 13.1 %copy-start.6 = (bf16[44,8,4,384]{3,1,2,0:T(8,128)(2,1)}, bf16[44,8,4,384]{3,1,2,0:T(8,128)(2,1)S(1)}, u32[]{:S(2)}) copy-start(bf16[44,8,4,384]{3,1,2,0:T(8,128)(2,1)S(1)} %copy.112) | copy-start | bytes 3244036
  163.4 4.6 %copy-start.11 = (bf16[1536,352]{1,0:T(8,128)(2,1)S(1)}, bf16[1536,352]{1,0:T(8,128)(2,1)}, u32[]{:S(2)}) copy-start(bf16[1536,352]{1,0:T(8,128)(2,1)} %gather_fusion.1) | copy-start | bytes 3244036
  163.4 4.6 %copy-start.14 = (bf16[352,1408]{1,0:T(8,128)(2,1)S(1)}, bf16[352,1408]{1,0:T(8,128)(2,1)}, u32[]{:S(2)}) copy-start(bf16[352,1408]{1,0:T(8,128)(2,1)} %reshape.326) | copy-start | bytes 2973700
  172.4 4.4 %copy-start.4 = (bf16[4,384,4,88]{1,0,3,2:T(4,128)(2,1)S(1)}, bf16[4,384,4,88]{1,0,3,2:T(4,128)(2,1)}, u32[]{:S(2)}) copy-start(bf16[4,384,4,88]{1,0,3,2:T(4,128)(2,1)} %reshape.322) | copy-start | bytes 3244036
  181.5 8.2 %copy-start.9 = (bf16[4,384,4,88]{1,0,3,2:T(4,128)(2,1)S(1)}, bf16[4,384,4,88]{1,0,3,2:T(4,128)(2,1)}, u32[]{:S(2)}) copy-start(bf16[4,384,4,88]{1,0,3,2:T(4,128)(2,1)} %reshape.323) | copy-start | bytes 3244036
  198.4 5.3 %copy-start.13 = (bf16[4,384,4,88]{1,3,2,0:T(8,128)(2,1)S(1)}, bf16[4,384,4,88]{1,3,2,0:T(8,128)(2,1)}, u32[]{:S(2)}) copy-start(bf16[4,384,4,88]{1,3,2,0:T(8,128)(2,1)} %fusion.37) | copy-start | bytes 3244036
  198.4 54.7 %all-to-all-start.2 = ((bf16[4,384,1408]{2,1,0:T(8,128)(2,1)}), bf16[4,384,1408]{2,1,0:T(8,128)(2,1)}, u32[]{:S(2)}, u32[]{:S(2)}) async-start(bf16[4,384,1408]{2,1,0:T(8,128)(2,1)} %bitcast.136), calls=%async_computation.2 | async-start | bytes 8650752 | tf_op jit(solution)/shard_map/all_to_all | solution.py:139
  203.4 101.0 %reduce-scatter.2.cloned.1.call-start = ((), (), s32[]{:S(2)}) async-start(), calls=%async_computation.9 | async-start | bytes 3649536 | tf_op jit(solution)/shard_map/reduce_scatter | solution.py:156
  203.7 1.2 copy-start.12
  253.1 32.9 %all-to-all-start.4 = ((bf16[8,44,1408]{2,1,0:T(8,128)(2,1)}), bf16[8,44,1408]{2,1,0:T(8,128)(2,1)}, u32[]{:S(2)}, u32[]{:S(2)}) async-start(bf16[8,44,1408]{2,1,0:T(8,128)(2,1)} %reshape.333), calls=%async_computation.5 | async-start | bytes 2162688 | tf_op jit(solution)/shard_map/all_to_all | solution.py:147
  286.0 55.6 %all-to-all-start.3 = ((bf16[4,384,1408]{2,1,0:T(8,128)(2,1)}), bf16[4,384,1408]{2,1,0:T(8,128)(2,1)}, u32[]{:S(2)}, u32[]{:S(2)}) async-start(bf16[4,384,1408]{2,1,0:T(8,128)(2,1)} %bitcast.135), calls=%async_computation.3 | async-start | bytes 8650752 | tf_op jit(solution)/shard_map/all_to_all | solution.py:174
  291.2 84.0 %all-gather.6.cloned.1.call-start = ((), (), s32[]{:S(2)}) async-start(), calls=%async_computation.10 | async-start | bytes 2478080 | tf_op jit(solution)/shard_map/all_gather | solution.py:158
  303.3 0.8 collective-permute-start.1
  306.3 3.2 copy-start.10
  306.3 3.2 copy-start.17
  346.9 16.3 %all-to-all-start.5 = ((f32[32,1,264]{2,1,0:T(1,128)}), f32[32,1,264]{2,1,0:T(1,128)S(1)}, u32[]{:S(2)}, u32[]{:S(2)}) async-start(f32[32,1,264]{2,1,0:T(1,128)} %all_to_all.30), calls=%async_computation.6 | async-start | bytes 98304 | tf_op jit(solution)/shard_map/all_to_all | solution.py:196
  363.9 9.8 %all-to-all-start.6 = ((f32[32,1,264]{2,1,0:T(1,128)}), f32[32,1,264]{2,1,0:T(1,128)S(1)}, u32[]{:S(2)}, u32[]{:S(2)}) async-start(f32[32,1,264]{2,1,0:T(1,128)} %broadcast_in_dim.58), calls=%async_computation.7 | async-start | bytes 98304 | tf_op jit(solution)/shard_map/all_to_all | solution.py:201
  (1 other events, 1.0 us)
Sparse Core Ops, SparseCore 0:
  11.9 84.7 all-gather.3
  217.3 85.9 reduce-scatter.1
  306.4 57.3 all-gather.5
